TPU v7x, 256 devices: a whole 4x4x8 slice. The times are simulated.
256 devices in a mesh: bx: 64 (over x, z, core), bz: 4 (over y).
Axes of the slice: x: 4, y: 4, z: 8, core: 2. Of those that a mesh axis runs over, the one named last changes fastest.
Arguments:
- fields: float32 [3, 512, 256, 512], P(None, 'bx', None, 'bz'), may hold values from 0.2 to 2
- conductance: float32 [512, 256, 512], P('bx', None, 'bz'), may hold values from 0.25 to 1
- absorption: float32 [512, 256, 512], P('bx', None, 'bz'), may hold values from 0.0001 to 0.01
- occupancy: int32 [64, 16, 16], P('bx', None, 'bz'), may hold values 0 or 1
- facing: int32 [16, 16], P(None, 'bz'), may hold values 0 or 1
Outputs:
- advanced: float32 [3, 512, 256, 512], P(None, 'bx', None, 'bz')
- picture: float32 [4, 256, 512], P(None, 'bx', 'bz')
All inputs are finite; a program needn't handle non-finite values. No bound on the sum of `occupancy` or of `facing` on one device may be relied on, other than what follows from the above.
Results may differ from a plain program's by a relative error of at most 0.00012.
Values sent between devices are 32-bit elements; how exact they have to be, the bound alone decides.
A program may use at most 128 MiB of HBM per device.

v0:
```python
import jax
import jax.numpy as jnp
from jax import lax
from jax.sharding import PartitionSpec as P

TY = 16
TZ = 32


def extended(cells, sides, width):
    for axis, dim in sides:
        count = lax.axis_size(axis)
        ends = count - 1
        head = lax.slice_in_dim(cells, 0, width, axis=dim)
        tail = lax.slice_in_dim(cells, cells.shape[dim] - width, cells.shape[dim], axis=dim)
        cells = jnp.concatenate(
            [
                lax.ppermute(tail, axis, [(i, (i + 1) % count) for i in range(ends)]),
                cells,
                lax.ppermute(head, axis, [((i + 1) % count, i) for i in range(ends)]),
            ],
            axis=dim,
        )
    return cells


def swapped(block, axis, distance):
    count = lax.axis_size(axis)
    route = []
    for low in range(count):
        high = low | 1 << distance
        if high != low and high < count:
            route += [(low, high), (high, low)]
    return lax.ppermute(block, axis, route)


def advance(padded):
    centre = padded[:, 1:-1, 1:-1, 1:-1]
    values = centre[:3]
    own = centre[3]
    neighbours = (
        padded[:, 2:, 1:-1, 1:-1],
        padded[:, :-2, 1:-1, 1:-1],
        padded[:, 1:-1, 2:, 1:-1],
        padded[:, 1:-1, :-2, 1:-1],
        padded[:, 1:-1, 1:-1, 2:],
        padded[:, 1:-1, 1:-1, :-2],
    )
    change = jnp.zeros_like(values)
    for beside in neighbours:
        change = change + 0.5 * (own + beside[3]) * (beside[:3] - values)
    return values + change / 7.0


def march(advanced, extinction):
    running = jnp.cumsum(extinction, axis=0)
    total = running[-1]
    ahead = running - extinction
    behind = total[None] - running
    glow = advanced * (1.0 - jnp.exp(-extinction))[None]
    front = jnp.sum(glow * jnp.exp(-ahead)[None], axis=1)
    back = jnp.sum(glow * jnp.exp(-behind)[None], axis=1)
    return (front, back, total)


def tile_map(flags, rows_each, cols_each):
    height = flags.shape[0]
    width = flags.shape[1]
    spread = jnp.broadcast_to(flags[:, None, :, None], (height, rows_each, width, cols_each))
    return spread.reshape(height * rows_each, width * cols_each).astype(jnp.float32)


def over_pair(lower, upper, flip):
    front_colour = lower[:3] + lower[3:] * upper[:3]
    back_colour = upper[:3] + upper[3:] * lower[:3]
    colour = jnp.where(flip > 0.5, back_colour, front_colour)
    return jnp.concatenate([colour, lower[3:] * upper[3:]], 0)


def shards(fields, conductance, absorption, occupancy, facing):
    height = fields.shape[2]
    across = fields.shape[3]
    stacked = jnp.concatenate([fields, conductance[None]], 0)
    padded = extended(stacked, (("bx", 1), ("bz", 3)), 1)
    padded = jnp.pad(padded, ((0, 0), (0, 0), (1, 1), (0, 0)))
    advanced = advance(padded)
    cell_mask = tile_map(occupancy[0], TY, TZ)
    extinction = absorption * advanced[0] * cell_mask[None]
    front, back, total = march(advanced, extinction)
    flip = tile_map(facing, TY, TZ)
    colour = jnp.where(flip > 0.5, back, front)
    image = jnp.concatenate([colour, jnp.exp(-total)[None]], 0)
    count = lax.axis_size("bx")
    position = lax.axis_index("bx")
    rounds = count.bit_length() - 1
    rows_each = height // count
    image = image.reshape(4, count, rows_each, across)
    flips = flip.reshape(count, rows_each, across)
    for level in range(rounds):
        pieces = image.shape[1]
        image = image.reshape(4, pieces // 2, 2, rows_each, across)
        flips = flips.reshape(pieces // 2, 2, rows_each, across)
        own_bit = position >> level & 1
        kept = lax.dynamic_index_in_dim(image, own_bit, 2, keepdims=False)
        given = lax.dynamic_index_in_dim(image, 1 - own_bit, 2, keepdims=False)
        flips = lax.dynamic_index_in_dim(flips, own_bit, 1, keepdims=False)
        partner = swapped(given, "bx", level)
        lower = jnp.where(own_bit == 0, kept, partner)
        upper = jnp.where(own_bit == 0, partner, kept)
        image = over_pair(lower, upper, flips)
    final = image[:, 0]
    picture = jnp.concatenate([final[:3], 1.0 - final[3:]], 0)
    return (advanced, picture)


def solution(mesh):
    placed = (
        P(None, "bx", None, "bz"),
        P("bx", None, "bz"),
        P("bx", None, "bz"),
        P("bx", None, "bz"),
        P(None, "bz"),
    )
    return jax.shard_map(
        shards,
        mesh=mesh,
        in_specs=placed,
        out_specs=(P(None, "bx", None, "bz"), P(None, "bx", "bz")),
        check_vma=False,
    )
```

profile of v0, /device:TPU:22, one launch (start us, length us, event | category | flops | bytes accessed | tf_op | source)
XLA Modules:
  0.0 124.9 jit_solution(39685973067354642)
XLA Ops:
  0.7 1.5 %pad_maximum_fusion.13 = (f32[4,1,256,128]{3,2,1,0:T(8,128)S(1)}, f32[4,1,256,128]{3,2,1,0:T(8,128)S(1)}) fusion(f32[1,8,256,128]{3,2,1,0:T(8,128)} %bitcast.95, f32[3,8,256,128]{3,2,1,0:T(8,128)} %param.5), kind=kLoop, calls=%fused_computation.70 | loop fusion | flops 262144 | bytes 5242880 | tf_op jit(solution)/shard_map/concatenate | solution.py:83
  2.1 7.6 %collective-permute-start = (f32[4,1,256,128]{3,2,1,0:T(8,128)S(1)}, f32[4,1,256,128]{3,2,1,0:T(8,128)S(1)}, u32[]{:S(2)}, u32[]{:S(2)}) collective-permute-start(f32[4,1,256,128]{3,2,1,0:T(8,128)S(1)} %get-tuple-element.21), channel_id=1, source_target_pairs={{4,0},{8,4},{12,8},{16,12},{20,16},{24,20},{28,24},{32,28},{36,32}... | collective-permute-start | bytes 1572872 | tf_op jit(solution)/shard_map/ppermute | solution.py:20
  9.7 1.9 %collective-permute-start.1 = (f32[4,1,256,128]{3,2,1,0:T(8,128)S(1)}, f32[4,1,256,128]{3,2,1,0:T(8,128)S(1)}, u32[]{:S(2)}, u32[]{:S(2)}) collective-permute-start(f32[4,1,256,128]{3,2,1,0:T(8,128)S(1)} %get-tuple-element.20), channel_id=1, source_target_pairs={{0,4},{4,8},{8,12},{12,16},{16,20},{20,24},{24,28},{28,32},{32,36}... | collective-permute-start | bytes 1572872 | tf_op jit(solution)/shard_map/ppermute | solution.py:18
  11.7 4.7 %collective-permute-done = f32[4,1,256,128]{3,2,1,0:T(8,128)S(1)} collective-permute-done((f32[4,1,256,128]{3,2,1,0:T(8,128)S(1)}, f32[4,1,256,128]{3,2,1,0:T(8,128)S(1)}, u32[]{:S(2)}, u32[]{:S(2)}) %collective-permute-start) | collective-permute-done | bytes 524320 | tf_op jit(solution)/shard_map/ppermute | solution.py:20
  16.4 5.9 %collective-permute-done.1 = f32[4,1,256,128]{3,2,1,0:T(8,128)S(1)} collective-permute-done((f32[4,1,256,128]{3,2,1,0:T(8,128)S(1)}, f32[4,1,256,128]{3,2,1,0:T(8,128)S(1)}, u32[]{:S(2)}, u32[]{:S(2)}) %collective-permute-start.1) | collective-permute-done | bytes 524320 | tf_op jit(solution)/shard_map/ppermute | solution.py:18
  22.8 5.9 %fusion.41 = (f32[4,10,256,1]{3,2,1,0:T(8,128)}, f32[4,10,256,1]{3,2,1,0:T(8,128)}) fusion(f32[4,10,256,128]{3,2,1,0:T(8,128)S(1)} %pad_maximum_fusion), kind=kLoop, calls=%fused_computation.146 | loop fusion | bytes 163840 | tf_op jit(solution)/shard_map/slice | solution.py:14
  28.6 4.2 %copy.64 = f32[4,10,256,1]{2,1,3,0:T(8,128)S(1)} copy(f32[4,10,256,1]{3,2,1,0:T(8,128)} %get-tuple-element.17) | data formatting | bytes 81920 | tf_op jit(solution)/shard_map/slice | solution.py:15
  32.8 3.3 %collective-permute-start.2 = (f32[4,10,256,1]{2,1,3,0:T(8,128)S(1)}, f32[4,10,256,1]{2,1,3,0:T(8,128)S(1)}, u32[]{:S(2)}, u32[]{:S(2)}) collective-permute-start(f32[4,10,256,1]{2,1,3,0:T(8,128)S(1)} %copy.64), channel_id=1, source_target_pairs={{0,1},{1,2},{2,3},{4,5},{5,6},{6,7},{8,9},{9,10},{10,11},{12,13},{... | collective-permute-start | bytes 122888 | tf_op jit(solution)/shard_map/ppermute | solution.py:18
  36.1 4.2 %copy.65 = f32[4,10,256,1]{2,1,3,0:T(8,128)S(1)} copy(f32[4,10,256,1]{3,2,1,0:T(8,128)} %get-tuple-element.16) | data formatting | bytes 81920 | tf_op jit(solution)/shard_map/slice | solution.py:14
  40.3 2.8 %collective-permute-start.3 = (f32[4,10,256,1]{2,1,3,0:T(8,128)S(1)}, f32[4,10,256,1]{2,1,3,0:T(8,128)S(1)}, u32[]{:S(2)}, u32[]{:S(2)}) collective-permute-start(f32[4,10,256,1]{2,1,3,0:T(8,128)S(1)} %copy.65), channel_id=1, source_target_pairs={{1,0},{2,1},{3,2},{5,4},{6,5},{7,6},{9,8},{10,9},{11,10},{13,12},{... | collective-permute-start | bytes 122888 | tf_op jit(solution)/shard_map/ppermute | solution.py:20
  44.0 3.1 %copy.66 = f32[4,10,256,1]{3,2,1,0:T(8,128)} copy(f32[4,10,256,1]{2,1,3,0:T(8,128)S(1)} %collective-permute-done.2) | data formatting | bytes 81920 | tf_op jit(solution)/shard_map/ppermute | solution.py:18
  47.0 3.1 %copy.67 = f32[4,10,256,1]{3,2,1,0:T(8,128)} copy(f32[4,10,256,1]{2,1,3,0:T(8,128)S(1)} %collective-permute-done.3) | data formatting | bytes 81920 | tf_op jit(solution)/shard_map/ppermute | solution.py:20
  50.2 13.7 %select_maximum_fusion = f32[4,10,258,130]{3,2,1,0:T(8,128)} fusion(f32[4,10,256,1]{3,2,1,0:T(8,128)} %copy.67, f32[4,10,256,1]{3,2,1,0:T(8,128)} %copy.66, f32[4,1,256,128]{3,2,1,0:T(8,128)S(1)} %collective-permute-done, f32[4,1,256,128]{3,2,1,0:T(8,128)S(1)} %collective-permute-done.1, f32[1,8,256,128]{3,2,1,0:T(8,128)S(1)} %bitcast.97, ...), kind=kLoop, calls=%fused_computation.2 | loop fusion | flops 18782400 | bytes 10691200 | tf_op jit(solution)/shard_map/concatenate | solution.py:16
  63.9 4.3 %fusion.27 = (f32[8,256,128]{2,1,0:T(8,128)}, f32[8,256,128]{2,1,0:T(8,128)}) fusion(f32[4,10,258,130]{3,2,1,0:T(8,128)} %select_maximum_fusion, f32[8,256,128]{2,1,0:T(8,128)S(1)} %copy-done.3), kind=kLoop, calls=%fused_computation.56 | loop fusion | flops 1048576 | bytes 5242880 | tf_op jit(solution)/shard_map/mul | solution.py:51
  68.2 2.8 %fusion.23 = (f32[8,256,128]{2,1,0:T(8,128)}, f32[8,256,128]{2,1,0:T(8,128)}, f32[8,256,128]{2,1,0:T(8,128)}, f32[8,256,128]{2,1,0:T(8,128)}) fusion(f32[1,8,256,128]{3,2,1,0:T(8,128)S(1)} %bitcast.98, f32[4,10,256,1]{3,2,1,0:T(8,128)S(1)} %copy-done, f32[4,1,256,128]{3,2,1,0:T(8,128)S(1)} %collective-permute-done, ...), kind=kLoop, calls=%fused_computation.50 | loop fusion | flops 5242880 | bytes 9519104 | tf_op jit(solution)/shard_map/mul | solution.py:51
  71.0 17.8 %fusion.5 = f32[3,8,256,128]{3,2,1,0:T(8,128)} fusion(f32[3,8,256,128]{3,2,1,0:T(8,128)} %param.5, f32[4,10,256,1]{3,2,1,0:T(8,128)} %copy.66, f32[4,1,256,128]{3,2,1,0:T(8,128)S(1)} %collective-permute-done, f32[4,1,256,128]{3,2,1,0:T(8,128)S(1)} %collective-permute-done.1, f32[1,8,256,128]{3,2,1,0:T(8,128)S(1)} %bitcast.99, f32[4,10,256,1]{3,2,1,0:T(8,128)} %copy.67, ...), kind=kLoop, calls=%fused_computation.14 | loop fusion | flops 24379392 | bytes 21053440 | tf_op jit(solution)/shard_map/add | solution.py:52
  88.8 1.4 %exponential_subtract_fusion = (f32[8,256,128]{2,1,0:T(8,128)S(1)}, f32[8,256,128]{2,1,0:T(8,128)S(1)}) fusion(f32[256,128]{1,0:T(8,128)S(1)} %convert_element_type.38, f32[8,256,128]{2,1,0:T(8,128)S(1)} %copy-done.5, f32[3,8,256,128]{3,2,1,0:T(8,128)} %fusion.5), kind=kLoop, calls=%fused_computation.65 | loop fusion | flops 1048576 | bytes 4325376 | tf_op jit(solution)/shard_map/sub | solution.py:60
  93.2 1.5 %collective-permute-done.4 = f32[4,32,4,128]{3,1,2,0:T(8,128)S(1)} collective-permute-done((f32[4,32,4,128]{3,1,2,0:T(8,128)S(1)}, f32[4,32,4,128]{3,1,2,0:T(8,128)S(1)}, u32[]{:S(2)}, u32[]{:S(2)}) %collective-permute-start.4) | collective-permute-done | bytes 262176 | tf_op jit(solution)/shard_map/ppermute | solution.py:34
  96.0 5.0 %collective-permute-done.5 = f32[4,16,4,128]{3,1,2,0:T(8,128)S(1)} collective-permute-done((f32[4,16,4,128]{3,1,2,0:T(8,128)S(1)}, f32[4,16,4,128]{3,1,2,0:T(8,128)S(1)}, u32[]{:S(2)}, u32[]{:S(2)}) %collective-permute-start.5) | collective-permute-done | bytes 131104 | tf_op jit(solution)/shard_map/ppermute | solution.py:34
  101.4 5.6 %collective-permute-done.6 = f32[4,8,4,128]{3,1,2,0:T(8,128)S(1)} collective-permute-done((f32[4,8,4,128]{3,1,2,0:T(8,128)S(1)}, f32[4,8,4,128]{3,1,2,0:T(8,128)S(1)}, u32[]{:S(2)}, u32[]{:S(2)}) %collective-permute-start.6) | collective-permute-done | bytes 65568 | tf_op jit(solution)/shard_map/ppermute | solution.py:34
  107.9 7.1 %collective-permute-done.7 = f32[4,4,4,128]{3,2,1,0:T(4,128)S(1)} collective-permute-done((f32[4,4,4,128]{3,2,1,0:T(4,128)S(1)}, f32[4,4,4,128]{3,2,1,0:T(4,128)S(1)}, u32[]{:S(2)}, u32[]{:S(2)}) %collective-permute-start.7) | collective-permute-done | bytes 32800 | tf_op jit(solution)/shard_map/ppermute | solution.py:34
  115.8 3.2 %collective-permute-done.8 = f32[4,2,4,128]{3,2,1,0:T(4,128)S(1)} collective-permute-done((f32[4,2,4,128]{3,2,1,0:T(4,128)S(1)}, f32[4,2,4,128]{3,2,1,0:T(4,128)S(1)}, u32[]{:S(2)}, u32[]{:S(2)}) %collective-permute-start.8) | collective-permute-done | bytes 16416 | tf_op jit(solution)/shard_map/ppermute | solution.py:34
  119.1 1.2 collective-permute-start.9
  120.2 4.1 %collective-permute-done.9 = f32[4,1,4,128]{3,2,1,0:T(4,128)S(1)} collective-permute-done((f32[4,1,4,128]{3,2,1,0:T(4,128)S(1)}, f32[4,1,4,128]{3,2,1,0:T(4,128)S(1)}, u32[]{:S(2)}, u32[]{:S(2)}) %collective-permute-start.9) | collective-permute-done | bytes 8224 | tf_op jit(solution)/shard_map/ppermute | solution.py:34
  (86 shorter events, 7.9 us)
Async XLA Ops:
  0.6 21.7 %copy-start.3 = (f32[8,256,128]{2,1,0:T(8,128)S(1)}, f32[8,256,128]{2,1,0:T(8,128)}, u32[]{:S(2)}) copy-start(f32[8,256,128]{2,1,0:T(8,128)} %param.6) | copy-start | bytes 3145732
  0.6 21.7 %copy-start.1 = (f32[3,8,256,128]{3,2,1,0:T(8,128)S(1)}, f32[3,8,256,128]{3,2,1,0:T(8,128)}, u32[]{:S(2)}) copy-start(f32[3,8,256,128]{3,2,1,0:T(8,128)} %param.5) | copy-start | bytes 9437188
  0.7 11.0 %copy-start.7 = (s32[1,16,4]{1,2,0:T(4,128)S(1)}, s32[1,16,4]{1,2,0:T(4,128)}, u32[]{:S(2)}) copy-start(s32[1,16,4]{1,2,0:T(4,128)} %param.8) | copy-start | bytes 772
  2.1 14.3 %collective-permute-start = (f32[4,1,256,128]{3,2,1,0:T(8,128)S(1)}, f32[4,1,256,128]{3,2,1,0:T(8,128)S(1)}, u32[]{:S(2)}, u32[]{:S(2)}) collective-permute-start(f32[4,1,256,128]{3,2,1,0:T(8,128)S(1)} %get-tuple-element.21), channel_id=1, source_target_pairs={{4,0},{8,4},{12,8},{16,12},{20,16},{24,20},{28,24},{32,28},{36,32}... | collective-permute-start | bytes 1572872 | tf_op jit(solution)/shard_map/ppermute | solution.py:20
  9.7 12.6 %collective-permute-start.1 = (f32[4,1,256,128]{3,2,1,0:T(8,128)S(1)}, f32[4,1,256,128]{3,2,1,0:T(8,128)S(1)}, u32[]{:S(2)}, u32[]{:S(2)}) collective-permute-start(f32[4,1,256,128]{3,2,1,0:T(8,128)S(1)} %get-tuple-element.20), channel_id=1, source_target_pairs={{0,4},{4,8},{8,12},{12,16},{16,20},{20,24},{24,28},{28,32},{32,36}... | collective-permute-start | bytes 1572872 | tf_op jit(solution)/shard_map/ppermute | solution.py:18
  32.8 10.3 %copy-start.6 = (s32[16,4]{0,1:T(4,128)S(1)}, s32[16,4]{0,1:T(4,128)}, u32[]{:S(2)}) copy-start(s32[16,4]{0,1:T(4,128)} %param.9) | copy-start | bytes 772
  32.8 11.1 %collective-permute-start.2 = (f32[4,10,256,1]{2,1,3,0:T(8,128)S(1)}, f32[4,10,256,1]{2,1,3,0:T(8,128)S(1)}, u32[]{:S(2)}, u32[]{:S(2)}) collective-permute-start(f32[4,10,256,1]{2,1,3,0:T(8,128)S(1)} %copy.64), channel_id=1, source_target_pairs={{0,1},{1,2},{2,3},{4,5},{5,6},{6,7},{8,9},{9,10},{10,11},{12,13},{... | collective-permute-start | bytes 122888 | tf_op jit(solution)/shard_map/ppermute | solution.py:18
  40.3 6.7 %collective-permute-start.3 = (f32[4,10,256,1]{2,1,3,0:T(8,128)S(1)}, f32[4,10,256,1]{2,1,3,0:T(8,128)S(1)}, u32[]{:S(2)}, u32[]{:S(2)}) collective-permute-start(f32[4,10,256,1]{2,1,3,0:T(8,128)S(1)} %copy.65), channel_id=1, source_target_pairs={{1,0},{2,1},{3,2},{5,4},{6,5},{7,6},{9,8},{10,9},{11,10},{13,12},{... | collective-permute-start | bytes 122888 | tf_op jit(solution)/shard_map/ppermute | solution.py:20
  47.0 21.1 %slice-start = ((s8[5242880]{0:T(1024)(128)(4,1)}), s8[1048576]{0:T(1024)(128)(4,1)S(1)}, s32[]{:S(2)}) async-start(s8[5242880]{0:T(1024)(128)(4,1)} %bitcast.93), calls=%async_computation | async-start | bytes 2097152
  50.1 18.0 %slice-start.1 = ((s8[5242880]{0:T(1024)(128)(4,1)}), s8[4194304]{0:T(1024)(128)(4,1)S(1)}, s32[]{:S(2)}) async-start(s8[5242880]{0:T(1024)(128)(4,1)} %bitcast.93), calls=%async_computation.1 | async-start | bytes 8388608
  50.1 18.0 %copy-start.2 = (f32[3,8,256,128]{3,2,1,0:T(8,128)S(1)}, f32[3,8,256,128]{3,2,1,0:T(8,128)}, u32[]{:S(2)}) copy-start(f32[3,8,256,128]{3,2,1,0:T(8,128)} %param.5) | copy-start | bytes 9437188
  63.9 4.3 %copy-start = (f32[4,10,256,1]{3,2,1,0:T(8,128)S(1)}, f32[4,10,256,1]{3,2,1,0:T(8,128)}, u32[]{:S(2)}) copy-start(f32[4,10,256,1]{3,2,1,0:T(8,128)} %copy.67) | copy-start | bytes 122884
  71.0 17.8 %copy-start.5 = (f32[8,256,128]{2,1,0:T(8,128)S(1)}, f32[8,256,128]{2,1,0:T(8,128)}, u32[]{:S(2)}) copy-start(f32[8,256,128]{2,1,0:T(8,128)} %param.7) | copy-start | bytes 3145732
  90.2 1.9 %copy-start.4 = (f32[3,8,256,128]{3,2,1,0:T(8,128)S(1)}, f32[3,8,256,128]{3,2,1,0:T(8,128)}, u32[]{:S(2)}) copy-start(f32[3,8,256,128]{3,2,1,0:T(8,128)} %fusion.5) | copy-start | bytes 9437188
  93.1 1.6 %collective-permute-start.4 = (f32[4,32,4,128]{3,1,2,0:T(8,128)S(1)}, f32[4,32,4,128]{3,1,2,0:T(8,128)S(1)}, u32[]{:S(2)}, u32[]{:S(2)}) collective-permute-start(f32[4,32,4,128]{3,1,2,0:T(8,128)S(1)} %bitcast.106), channel_id=1, source_target_pairs={{0,4},{4,0},{8,12},{12,8},{16,20},{20,16},{24,28},{28,24},{32,36},... | collective-permute-start | bytes 786440 | tf_op jit(solution)/shard_map/ppermute | solution.py:34
  95.2 5.8 %collective-permute-start.5 = (f32[4,16,4,128]{3,1,2,0:T(8,128)S(1)}, f32[4,16,4,128]{3,1,2,0:T(8,128)S(1)}, u32[]{:S(2)}, u32[]{:S(2)}) collective-permute-start(f32[4,16,4,128]{3,1,2,0:T(8,128)S(1)} %bitcast.111), channel_id=1, source_target_pairs={{0,8},{8,0},{4,12},{12,4},{16,24},{24,16},{20,28},{28,20},{32,40},... | collective-permute-start | bytes 393224 | tf_op jit(solution)/shard_map/ppermute | solution.py:34
  101.3 5.7 %collective-permute-start.6 = (f32[4,8,4,128]{3,1,2,0:T(8,128)S(1)}, f32[4,8,4,128]{3,1,2,0:T(8,128)S(1)}, u32[]{:S(2)}, u32[]{:S(2)}) collective-permute-start(f32[4,8,4,128]{3,1,2,0:T(8,128)S(1)} %bitcast.112), channel_id=1, source_target_pairs={{0,16},{16,0},{4,20},{20,4},{8,24},{24,8},{12,28},{28,12},{32,48},... | collective-permute-start | bytes 196616 | tf_op jit(solution)/shard_map/ppermute | solution.py:34
  107.2 7.9 %collective-permute-start.7 = (f32[4,4,4,128]{3,2,1,0:T(4,128)S(1)}, f32[4,4,4,128]{3,2,1,0:T(4,128)S(1)}, u32[]{:S(2)}, u32[]{:S(2)}) collective-permute-start(f32[4,4,4,128]{3,2,1,0:T(4,128)S(1)} %bitcast.113), channel_id=1, source_target_pairs={{0,32},{32,0},{4,36},{36,4},{8,40},{40,8},{12,44},{44,12},{16,48},... | collective-permute-start | bytes 98312 | tf_op jit(solution)/shard_map/ppermute | solution.py:34
  115.2 3.8 %collective-permute-start.8 = (f32[4,2,4,128]{3,2,1,0:T(4,128)S(1)}, f32[4,2,4,128]{3,2,1,0:T(4,128)S(1)}, u32[]{:S(2)}, u32[]{:S(2)}) collective-permute-start(f32[4,2,4,128]{3,2,1,0:T(4,128)S(1)} %dynamic-slice_bitcast_fusion), channel_id=1, source_target_pairs={{0,64},{64,0},{4,68},{68,4},{8,72},{72,8},{12,76},{76,12},{16,80},... | collective-permute-start | bytes 49160 | tf_op jit(solution)/shard_map/ppermute | solution.py:34
  119.1 5.2 %collective-permute-start.9 = (f32[4,1,4,128]{3,2,1,0:T(4,128)S(1)}, f32[4,1,4,128]{3,2,1,0:T(4,128)S(1)}, u32[]{:S(2)}, u32[]{:S(2)}) collective-permute-start(f32[4,1,4,128]{3,2,1,0:T(4,128)S(1)} %fusion.35), channel_id=1, source_target_pairs={{0,128},{128,0},{4,132},{132,4},{8,136},{136,8},{12,140},{140,12},... | collective-permute-start | bytes 24584 | tf_op jit(solution)/shard_map/ppermute | solution.py:34
where the time goes:
time: 125 us
  other arithmetic  45 us (36%)
  waiting for transfers between devices  37.2 us (30%)
  local copies, waits for them, and re-layouts  22.8 us (18%)
  starting transfers between devices  18.7 us (15%)
    ppermute x6, waiting for transfers between devices, swapped(): return lax.ppermute(block, axis, route)  26.6 us
    add x1, other arithmetic, advance(): return values + change / 7.0  17.8 us
    concatenate x2, other arithmetic, extended(): jnp.concatenate([lax.ppermute(tail, axis, [(i, (i + 1) % count) for i in...  14.1 us
    ppermute x2, starting transfers between devices, extended(): lax.ppermute(head, axis, [((i + 1) % count, i) for i in range(ends)])  10.4 us
    slice x2, local copies, waits for them, and re-layouts, extended(): head = lax.slice_in_dim(cells, 0, width, axis=dim)  10 us
    mul x2, other arithmetic, advance(): change = change + 0.5 * (own + beside[3]) * (beside[:3] - values)  7.1 us
    ppermute x2, waiting for transfers between devices, extended(): lax.ppermute(tail, axis, [(i, (i + 1) % count) for i in range(ends)])  5.93 us
    ppermute x2, starting transfers between devices, extended(): lax.ppermute(tail, axis, [(i, (i + 1) % count) for i in range(ends)])  5.25 us
  transfers between devices with their start and end apart: 10, of which 8 were waited for; matrix products, arithmetic and copies ran while one was open for 7% of the time, Pallas kernels for 0%

commit v1 on v0

v1 whole, which is shorter than its diff:
```python
import functools

import jax
import jax.numpy as jnp
from jax import lax
from jax.experimental import pallas as pl
from jax.experimental.pallas import tpu as pltpu
from jax.sharding import PartitionSpec as P

MESH = pl.DeviceIdType.MESH
TY = 16
TZ = 32
ZS = 8
PAD = 8


def tile_lanes(flag, row, lane):
    out = jnp.where(lane < TZ, flag(row, 0), flag(row, 1))
    out = jnp.where(lane < 2 * TZ, out, flag(row, 2))
    return jnp.where(lane < 3 * TZ, out, flag(row, 3)).astype(jnp.float32)


def kernel(
    n_bx, n_bz, cx, ny,
    fields, cond, absn, occ, facing,
    adv, pic,
    u, k, ab, lo_u, lo_k, hi_u, hi_k, zs, zl, zr, occ_m, fac_m, pair, give, ready, got,
    in_sem, hs_sem, hr_sem, zs_sem, zr_sem, cs_sem, cr_sem, as_sem, ar_sem,
):
    xs = n_bx // (2 * ZS)
    nb = xs
    rows = ny // nb
    groups = rows // 8
    bx = lax.axis_index("bx")
    bz = lax.axis_index("bz")
    core = bx % 2
    z = (bx // 2) % ZS
    x = bx // (2 * ZS)
    has_lo, has_hi = bx > 0, bx < n_bx - 1
    has_l, has_r = bz > 0, bz < n_bz - 1
    lo_id, hi_id = (bx - 1, bz), (bx + 1, bz)
    l_id, r_id = (bx, bz - 1), (bx, bz + 1)
    lo_x = (bx - 1) // (2 * ZS)
    hi_x = (bx + 1) // (2 * ZS)
    mate = (bx + 1 - 2 * core, bz)

    def start_row(of_x, b):
        return pl.multiple_of(((of_x + b) % nb) * rows, rows)

    def chip_id(dx, dz):
        return ((((x + dx) % xs) * ZS + (z + dz) % ZS) * 2 + core, bz)

    barrier = pltpu.get_barrier_semaphore()

    def greet(who):
        pl.semaphore_signal(barrier, inc=1, device_id=who, device_id_type=MESH)

    for dx in range(xs):
        for dz in range(ZS):
            if (dx, dz) != (0, 0):
                greet(chip_id(dx, dz))
    for cond_, who in ((has_lo, lo_id), (has_hi, hi_id), (has_l, l_id), (has_r, r_id)):
        @pl.when(cond_)
        def _():
            greet(who)

    def loads(b):
        at = pl.ds(start_row(x, b), rows)
        to = pl.ds(start_row(x, b) + PAD, rows)
        return (
            pltpu.make_async_copy(fields.at[:, :, at, :], u.at[:, :, to, :], in_sem.at[b, 0]),
            pltpu.make_async_copy(cond.at[:, at, :], k.at[:, to, :], in_sem.at[b, 1]),
            pltpu.make_async_copy(absn.at[:, at, :], ab.at[:, at, :], in_sem.at[b, 2]),
        )

    for b in range(nb):
        for c in loads(b):
            c.start()

    for p in range(cx):
        k[p, 0:PAD, :] = jnp.zeros((PAD, 128), jnp.float32)
        k[p, PAD + ny : 2 * PAD + ny, :] = jnp.zeros((PAD, 128), jnp.float32)
        for a in range(3):
            u[a, p, 0:PAD, :] = jnp.zeros((PAD, 128), jnp.float32)
            u[a, p, PAD + ny : 2 * PAD + ny, :] = jnp.zeros((PAD, 128), jnp.float32)

    @pl.when(bx == 0)
    def _():
        lo_u[...] = jnp.zeros_like(lo_u)
        lo_k[...] = jnp.zeros_like(lo_k)

    @pl.when(bx == n_bx - 1)
    def _():
        hi_u[...] = jnp.zeros_like(hi_u)
        hi_k[...] = jnp.zeros_like(hi_k)

    @pl.when(bz == 0)
    def _():
        zl[...] = jnp.zeros_like(zl)

    @pl.when(bz == n_bz - 1)
    def _():
        zr[...] = jnp.zeros_like(zr)

    lane = lax.broadcasted_iota(jnp.int32, (8, 128), 1)
    lane1 = lax.broadcasted_iota(jnp.int32, (1, 128), 1)
    for t in range(ny // TY):
        occ_m[t : t + 1, :] = tile_lanes(lambda i, j: occ[0, i, j], t, lane1)
        fac_m[t : t + 1, :] = tile_lanes(lambda i, j: facing[i, j], t, lane1)

    pl.semaphore_wait(
        barrier,
        xs * ZS - 1 + has_lo.astype(jnp.int32) + has_hi.astype(jnp.int32)
        + has_l.astype(jnp.int32) + has_r.astype(jnp.int32),
    )

    def halo(b, up):
        of_x, who, p = (hi_x, hi_id, cx - 1) if up else (lo_x, lo_id, 0)
        to_u, to_k = (lo_u, lo_k) if up else (hi_u, hi_k)
        at = pl.ds(start_row(of_x, b), rows)
        d = int(up)
        return (
            pltpu.make_async_remote_copy(
                fields.at[:, p, at, :], to_u.at[:, at, :], hs_sem.at[b, d, 0], hr_sem.at[b, d, 0],
                device_id=who, device_id_type=MESH),
            pltpu.make_async_remote_copy(
                cond.at[p, at, :], to_k.at[at, :], hs_sem.at[b, d, 1], hr_sem.at[b, d, 1],
                device_id=who, device_id_type=MESH),
        )

    for b in range(nb):
        @pl.when(has_lo)
        def _():
            for c in halo(b, False):
                c.start()

        @pl.when(has_hi)
        def _():
            for c in halo(b, True):
                c.start()

    slot = ((lane + 1) % 128) // 2

    def edge(b, right):
        return pltpu.make_async_remote_copy(
            zs.at[b], (zl if right else zr).at[b], zs_sem.at[b, int(right)], zr_sem.at[b, int(right)],
            device_id=r_id if right else l_id, device_id_type=MESH)

    def pack_batch(b, carry):
        for c in loads(b):
            c.wait()
        r0 = start_row(x, b)

        def pack(g, carry):
            at = pl.ds(pl.multiple_of(r0 + g * 8, 8) + PAD, 8)
            out = jnp.zeros((8, 128), jnp.float32)
            for p in range(cx):
                for a in range(4):
                    j = p * 4 + a
                    v = k[p, at, :] if a == 3 else u[a, p, at, :]
                    if j:
                        v = pltpu.roll(v, 2 * j, 1)
                    out = jnp.where(slot == j, v, out)
            zs[b, pl.ds(pl.multiple_of(g * 8, 8), 8), :] = out
            return carry

        lax.fori_loop(0, groups, pack, 0)

        @pl.when(has_l)
        def _():
            edge(b, False).start()

        @pl.when(has_r)
        def _():
            edge(b, True).start()

        return carry

    lax.fori_loop(0, nb, pack_batch, 0)

    def core_copy(b):
        return pltpu.make_async_remote_copy(
            give.at[b], pair.at[b, core], cs_sem.at[b], cr_sem.at[b], device_id=mate, device_id_type=MESH)

    def send_out(b, e):
        far = 4 + ((e + 1) // 2) * (2 * (e % 2) - 1)
        dest = (z + far) % ZS
        return dest, pltpu.make_async_remote_copy(
            ready.at[b, dest], got.at[x * ZS + z], as_sem.at[b, e], ar_sem.at[x * ZS + z],
            device_id=chip_id(b, far), device_id_type=MESH)

    def wait_halo(b):
        @pl.when(has_lo)
        def _():
            for c in halo(b, True):
                c.wait_recv()

        @pl.when(has_hi)
        def _():
            for c in halo(b, False):
                c.wait_recv()

        @pl.when(has_l)
        def _():
            edge(b, True).wait_recv()

        @pl.when(has_r)
        def _():
            edge(b, False).wait_recv()

    def work(b):
        wait_halo(b)
        r0 = start_row(x, b)

        def step(g, carry):
            y0 = pl.multiple_of(r0 + g * 8, 8)
            at = pl.ds(y0, 8)
            mid = pl.ds(y0 + PAD, 8)
            above = pl.ds(y0 + PAD + 1, 8)
            below = pl.ds(y0 + PAD - 1, 8)
            here = pl.ds(pl.multiple_of(g * 8, 8), 8)
            edges = jnp.where(lane % 2 == 0, zr[b, here, :], pltpu.roll(zl[b, here, :], 2, 1))
            tile = y0 // TY
            mask = occ_m[pl.ds(tile, 1), :]
            flip = jnp.broadcast_to(fac_m[pl.ds(tile, 1), :] > 0.5, (8, 128))
            first, last = lane == 0, lane == 127

            k_prev = lo_k[at, :]
            u_prev = [lo_u[a, at, :] for a in range(3)]
            k_here = k[0, mid, :]
            u_here = [u[a, 0, mid, :] for a in range(3)]
            flow = [(k_prev + k_here) * (u_prev[a] - u_here[a]) for a in range(3)]
            through = jnp.ones((8, 128), jnp.float32)
            colour = [jnp.zeros((8, 128), jnp.float32)] * 3
            for p in range(cx):
                if p < cx - 1:
                    k_next = k[p + 1, mid, :]
                    u_next = [u[a, p + 1, mid, :] for a in range(3)]
                else:
                    k_next = hi_k[at, :]
                    u_next = [hi_u[a, at, :] for a in range(3)]
                k_x = k_here + k_next
                k_a = k_here + k[p, above, :]
                k_b = k_here + k[p, below, :]
                e = pltpu.roll(edges, 127 - 2 * (p * 4 + 3), 1)
                k_l = k_here + jnp.where(first, e, pltpu.roll(k_here, 1, 1))
                k_r = k_here + jnp.where(last, e, pltpu.roll(k_here, 127, 1))
                new = []
                for a in range(3):
                    v = u_here[a]
                    next_flow = k_x * (u_next[a] - v)
                    change = flow[a] + next_flow
                    change = change + k_a * (u[a, p, above, :] - v)
                    change = change + k_b * (u[a, p, below, :] - v)
                    e = pltpu.roll(edges, 127 - 2 * (p * 4 + a), 1)
                    change = change + k_l * (jnp.where(first, e, pltpu.roll(v, 1, 1)) - v)
                    change = change + k_r * (jnp.where(last, e, pltpu.roll(v, 127, 1)) - v)
                    flow[a] = -next_flow
                    out = v + change * (0.5 / 7.0)
                    adv[a, p, at, :] = out
                    new.append(out)
                extinction = ab[p, at, :] * new[0] * mask
                passed = jnp.exp(-extinction)
                glow = (1.0 - passed) * jnp.where(flip, 1.0, through)
                keep = jnp.where(flip, passed, 1.0)
                colour = [colour[a] * keep + new[a] * glow for a in range(3)]
                through = through * passed
                k_here, u_here = k_next, u_next
            for c, v in enumerate(colour + [through]):
                top, bottom = v[0:4], v[4:8]
                pair[b, core, g, c] = jnp.where(core == 0, top, bottom)
                give[b, g, c] = jnp.where(core == 0, bottom, top)
            return carry

        lax.fori_loop(0, groups, step, 0)
        core_copy(b).start()

    def merge(b):
        core_copy(b).wait_recv()
        tile0 = (start_row(x, b) // TY)

        def step(g, carry):
            flip = jnp.broadcast_to(fac_m[pl.ds(tile0 + g // 2, 1), :] > 0.5, (4, 128))
            t0, t1 = pair[b, 0, g, 3], pair[b, 1, g, 3]
            for c in range(3):
                c0, c1 = pair[b, 0, g, c], pair[b, 1, g, c]
                ready[b, g, c] = jnp.where(flip, c1 + t1 * c0, c0 + t0 * c1)
            ready[b, g, 3] = t0 * t1
            return carry

        lax.fori_loop(0, groups, step, 0)
        for e in range(ZS):
            _, c = send_out(b, e)
            if e < ZS - 1:
                c.start()
            else:
                @pl.when(b > 0)
                def _():
                    c.start()

    def batch(b, carry):
        @pl.when(b < nb)
        def _():
            work(b)

        @pl.when(b > 0)
        def _():
            merge(b - 1)

        return carry

    lax.fori_loop(0, nb + 1, batch, 0)

    flip = jnp.broadcast_to(fac_m[pl.ds(bx * 4 // TY, 1), :] > 0.5, (4, 128))
    me = x * ZS + z
    got[pl.ds(me, 1)] = ready[0, pl.ds(z, 1)]

    def gather(s, carry):
        colour, through = carry[:3], carry[3]

        @pl.when(s != me)
        def _():
            pltpu.make_async_remote_copy(
                ready.at[0, 0], got.at[s], as_sem.at[0, 0], ar_sem.at[s],
                device_id=mate, device_id_type=MESH).wait_recv()

        t = got[s, 3]
        colour = [
            jnp.where(flip, got[s, c] + t * colour[c], colour[c] + through * got[s, c]) for c in range(3)
        ]
        return (*colour, through * t)

    zero = jnp.zeros((4, 128), jnp.float32)
    out = lax.fori_loop(0, xs * ZS, gather, (zero, zero, zero, jnp.ones((4, 128), jnp.float32)))
    for c in range(3):
        pic[c] = out[c]
    pic[3] = 1.0 - out[3]

    def drain(b, carry):
        @pl.when(has_lo)
        def _():
            for c in halo(b, False):
                c.wait_send()

        @pl.when(has_hi)
        def _():
            for c in halo(b, True):
                c.wait_send()

        @pl.when(has_l)
        def _():
            edge(b, False).wait_send()

        @pl.when(has_r)
        def _():
            edge(b, True).wait_send()

        core_copy(b).wait_send()
        for e in range(ZS):
            _, c = send_out(b, e)
            if e < ZS - 1:
                c.wait_send()
            else:
                @pl.when(b > 0)
                def _():
                    c.wait_send()
        return carry

    lax.fori_loop(0, nb, drain, 0)


def solution(mesh):
    n_bx, n_bz = mesh.shape["bx"], mesh.shape["bz"]

    def shards(fields, conductance, absorption, occupancy, facing):
        _, cx, ny, nz = fields.shape
        xs = n_bx // (2 * ZS)
        nb, rows = xs, ny // xs
        f32 = jnp.float32
        vmem, dma = pltpu.VMEM, pltpu.SemaphoreType.DMA
        hbm = pl.BlockSpec(memory_space=pl.ANY)
        smem = pl.BlockSpec(memory_space=pltpu.SMEM)
        in_vmem = pl.BlockSpec(memory_space=pltpu.VMEM)
        return pl.pallas_call(
            functools.partial(kernel, n_bx, n_bz, cx, ny),
            out_shape=(
                jax.ShapeDtypeStruct(fields.shape, f32),
                jax.ShapeDtypeStruct((4, ny // n_bx, nz), f32),
            ),
            in_specs=[hbm, hbm, hbm, smem, smem],
            out_specs=(in_vmem, in_vmem),
            scratch_shapes=[
                vmem((3, cx, ny + 2 * PAD, nz), f32),
                vmem((cx, ny + 2 * PAD, nz), f32),
                vmem((cx, ny, nz), f32),
                vmem((3, ny, nz), f32),
                vmem((ny, nz), f32),
                vmem((3, ny, nz), f32),
                vmem((ny, nz), f32),
                vmem((nb, rows, nz), f32),
                vmem((nb, rows, nz), f32),
                vmem((nb, rows, nz), f32),
                vmem((ny // TY, nz), f32),
                vmem((ny // TY, nz), f32),
                vmem((nb, 2, rows // 8, 4, 4, nz), f32),
                vmem((nb, rows // 8, 4, 4, nz), f32),
                vmem((nb, rows // 8, 4, 4, nz), f32),
                vmem((xs * ZS, 4, 4, nz), f32),
                dma((nb, 3)),
                dma((nb, 2, 2)),
                dma((nb, 2, 2)),
                dma((nb, 2)),
                dma((nb, 2)),
                dma((nb,)),
                dma((nb,)),
                dma((nb, ZS)),
                dma((xs * ZS,)),
            ],
            compiler_params=pltpu.CompilerParams(
                collective_id=0, has_side_effects=True, vmem_limit_bytes=30 << 20
            ),
            name="step_and_render",
        )(fields, conductance, absorption, occupancy, facing)

    return jax.shard_map(
        shards,
        mesh=mesh,
        in_specs=(
            P(None, "bx", None, "bz"),
            P("bx", None, "bz"),
            P("bx", None, "bz"),
            P("bx", None, "bz"),
            P(None, "bz"),
        ),
        out_specs=(P(None, "bx", None, "bz"), P(None, "bx", "bz")),
        check_vma=False,
    )
```

time: 125 us -> 38.7 us (0.31)
  the two profiles are of different devices: /device:TPU:22 before, /device:TPU:1 now
where the time goes in v1:
time: 38.7 us; the launch traced here: 38.5 us
  Pallas kernels  29.7 us (77%)
  local copies, waits for them, and re-layouts  8.12 us (21%)
  between operations  0.64 us (2%)
    pallas_call x1, Pallas kernels, shards(): pl.pallas_call(functools.partial(kernel, n_bx, n_bz, cx, ny), out_shape=(...  29.7 us
    unnamed x10, local copies, waits for them, and re-layouts  8.12 us

profile of v1, /device:TPU:1, one launch (start us, length us, event | category | flops | bytes accessed | tf_op | source)
XLA Modules:
  0.0 38.5 jit_solution(8054893222477264715)
XLA Ops:
  0.6 0.8 %copy.7.occ = s32[1,16,4]{2,1,0:T(8,128)S(1)} copy(s32[1,16,4]{1,2,0:T(4,128)} %param.8) | data formatting | bytes 512 | tf_op args[3]
  1.4 0.8 %copy.8.facing = s32[16,4]{1,0:T(8,128)S(1)} copy(s32[16,4]{0,1:T(4,128)} %param.9) | data formatting | bytes 512 | tf_op args[4]
  2.1 0.0 copy-start
  2.1 1.9 %copy-done = f32[3,8,256,128]{3,2,1,0:T(8,128)S(1)} copy-done((f32[3,8,256,128]{3,2,1,0:T(8,128)S(1)}, f32[3,8,256,128]{3,2,1,0:T(8,128)}, u32[]{:S(2)}) %copy-start) | copy-done | bytes 3145752
  4.0 0.0 copy-start.1
  4.0 1.2 %copy-done.1 = f32[8,256,128]{2,1,0:T(8,128)S(1)} copy-done((f32[8,256,128]{2,1,0:T(8,128)S(1)}, f32[8,256,128]{2,1,0:T(8,128)}, u32[]{:S(2)}) %copy-start.1) | copy-done | bytes 1048600
  5.3 0.0 copy-start.2
  5.3 1.2 %copy-done.2 = f32[8,256,128]{2,1,0:T(8,128)S(1)} copy-done((f32[8,256,128]{2,1,0:T(8,128)S(1)}, f32[8,256,128]{2,1,0:T(8,128)}, u32[]{:S(2)}) %copy-start.2) | copy-done | bytes 1048600
  6.5 29.7 %step_and_render.1 = (f32[3,8,256,128]{3,2,1,0:T(8,128)S(1)}, f32[4,4,128]{2,1,0:T(4,128)S(1)}) custom-call(f32[3,8,256,128]{3,2,1,0:T(8,128)S(1)} %copy-done, f32[8,256,128]{2,1,0:T(8,128)S(1)} %copy-done.1, f32[8,256,128]{2,1,0:T(8,128)S(1)} %copy-done.2, s32[1,16,4]{2,1,0:T(8,128)S(1)} %copy.7.occ, s32[16,4]{1,0:T(8,128)S(1)} %copy.8.facing), custom_call_target="tpu_custom_call" | custom-call | tf_op jit(solution)/shard_map/step_and_render/pallas_call | solution.py:384
  36.2 1.7 %copy.11 = f32[3,8,256,128]{3,2,1,0:T(8,128)} copy(f32[3,8,256,128]{3,2,1,0:T(8,128)S(1)} %get-tuple-element.4) | data formatting | bytes 6291456
  37.9 0.6 %copy.12 = f32[4,4,128]{2,1,0:T(4,128)} copy(f32[4,4,128]{2,1,0:T(4,128)S(1)} %get-tuple-element.5) | data formatting | bytes 16384
Async XLA Ops:
  2.1 1.9 %copy-start = (f32[3,8,256,128]{3,2,1,0:T(8,128)S(1)}, f32[3,8,256,128]{3,2,1,0:T(8,128)}, u32[]{:S(2)}) copy-start(f32[3,8,256,128]{3,2,1,0:T(8,128)} %fields.1) | copy-start | bytes 9437188
  4.0 1.2 %copy-start.1 = (f32[8,256,128]{2,1,0:T(8,128)S(1)}, f32[8,256,128]{2,1,0:T(8,128)}, u32[]{:S(2)}) copy-start(f32[8,256,128]{2,1,0:T(8,128)} %cond.1) | copy-start | bytes 3145732
  5.3 1.2 %copy-start.2 = (f32[8,256,128]{2,1,0:T(8,128)S(1)}, f32[8,256,128]{2,1,0:T(8,128)}, u32[]{:S(2)}) copy-start(f32[8,256,128]{2,1,0:T(8,128)} %absn.1) | copy-start | bytes 3145732

commit v2 on v1

v2 whole, which is shorter than its diff:
```python
import functools

import jax
import jax.numpy as jnp
from jax import lax
from jax.experimental import pallas as pl
from jax.experimental.pallas import tpu as pltpu
from jax.sharding import PartitionSpec as P

MESH = pl.DeviceIdType.MESH
TY = 16
TZ = 32
ZS = 8
PAD = 8
LIMIT = 30 << 20
SHARE = 0.5 / 7.0
PU, AU, BU = 2, 2, 2
EARLY = 2
NB = 4


def spread(flags):
    column = lax.broadcasted_iota(jnp.int32, (flags.shape[0], 128), 0)
    lane = lax.broadcasted_iota(jnp.int32, (flags.shape[0], 128), 1)
    own = (lane // TZ == column).astype(jnp.float32)
    return lax.dot_general(
        flags.astype(jnp.float32), own, (((0,), (0,)), ((), ())), preferred_element_type=jnp.float32
    )


def kernel(
    n_bx, n_bz, cx, ny,
    fields, cond, absn, occ, facing,
    adv, pic,
    u, k, ab, lo_u, lo_k, hi_u, hi_k, zs, zl, zr, occ_m, fac_m, pair, give, ready, got, flags,
    word, flag_sem, in_sem, hs_sem, hr_sem, zs_sem, zr_sem, cs_sem, cr_sem, as_sem, ar_sem,
):
    xs = n_bx // (2 * ZS)
    nb = NB
    m = xs // nb
    rows = ny // nb
    groups = rows // 8
    bx = lax.axis_index("bx")
    bz = lax.axis_index("bz")
    core = bx % 2
    z = (bx // 2) % ZS
    x = bx // (2 * ZS)
    has_lo, has_hi = bx > 0, bx < n_bx - 1
    has_l, has_r = bz > 0, bz < n_bz - 1
    lo_id, hi_id = (bx - 1, bz), (bx + 1, bz)
    l_id, r_id = (bx, bz - 1), (bx, bz + 1)
    lo_x = (bx - 1) // (2 * ZS)
    hi_x = (bx + 1) // (2 * ZS)
    mate = (bx + 1 - 2 * core, bz)

    def start_row(of_x, b):
        return pl.multiple_of(((of_x // m + b) % nb) * rows, rows)

    def chip_id(dx, dz):
        return ((((x + dx) % xs) * ZS + (z + dz) % ZS) * 2 + core, bz)

    barrier = pltpu.get_barrier_semaphore()
    line = [(0, dz) for dz in (1, ZS - 1, 2, ZS - 2, 3, ZS - 3, 4)] + [(dx, 0) for dx in range(1, xs)]

    def greet(sem, who):
        pl.semaphore_signal(sem, inc=1, device_id=who, device_id_type=MESH)

    for near, who in ((has_lo, lo_id), (has_hi, hi_id), (has_l, l_id), (has_r, r_id)):
        @pl.when(near)
        def _():
            greet(barrier, who)
    for dx, dz in line:
        greet(barrier, chip_id(dx, dz))

    def loads(b):
        at = pl.ds(start_row(x, b), rows)
        to = pl.ds(start_row(x, b) + PAD, rows)
        return (
            pltpu.make_async_copy(fields.at[:, :, at, :], u.at[:, :, to, :], in_sem.at[b, 0]),
            pltpu.make_async_copy(cond.at[:, at, :], k.at[:, to, :], in_sem.at[b, 1]),
            pltpu.make_async_copy(absn.at[:, at, :], ab.at[:, at, :], in_sem.at[b, 2]),
        )

    for b in range(nb):
        for c in loads(b)[:2]:
            c.start()
    for b in range(nb):
        loads(b)[2].start()

    lane = lax.broadcasted_iota(jnp.int32, (flags.shape[0], 128), 1)
    own = (lane // TZ == column).astype(jnp.float32)
    return lax.dot_general(
        flags.astype(jnp.float32), own, (((0,), (0,)), ((), ())), preferred_element_type=jnp.float32
    )


def kernel(
    n_bx, n_bz, cx, ny,
    fields, cond, absn, occ, facing,
    adv, pic,
    u, k, ab, lo_u, lo_k, hi_u, hi_k, zs, zl, zr, occ_m, fac_m, pair, give, ready, got, flags,
    word, flag_sem, in_sem, hs_sem, hr_sem, zs_sem, zr_sem, cs_sem, cr_sem, as_sem, ar_sem,
):
    xs = n_bx // (2 * ZS)
    nb = NB
    m = xs // nb
    rows = ny // nb
    groups = rows // 8
    bx = lax.axis_index("bx")
    bz = lax.axis_index("bz")
    core = bx % 2
    z = (bx // 2) % ZS
    x = bx // (2 * ZS)
    has_lo, has_hi = bx > 0, bx < n_bx - 1
    has_l, has_r = bz > 0, bz < n_bz - 1
    lo_id, hi_id = (bx - 1, bz), (bx + 1, bz)
    l_id, r_id = (bx, bz - 1), (bx, bz + 1)
    lo_x = (bx - 1) // (2 * ZS)
    hi_x = (bx + 1) // (2 * ZS)
    mate = (bx + 1 - 2 * core, bz)

    def start_row(of_x, b):
        return pl.multiple_of(((of_x // m + b) % nb) * rows, rows)

    def chip_id(dx, dz):
        return ((((x + dx) % xs) * ZS + (z + dz) % ZS) * 2 + core, bz)

    barrier = pltpu.get_barrier_semaphore()
    line = [(0, dz) for dz in (1, ZS - 1, 2, ZS - 2, 3, ZS - 3, 4)] + [(dx, 0) for dx in range(1, xs)]

    def greet(sem, who):
        pl.semaphore_signal(sem, inc=1, device_id=who, device_id_type=MESH)

    for near, who in ((has_lo, lo_id), (has_hi, hi_id), (has_l, l_id), (has_r, r_id)):
        @pl.when(near)
        def _():
            greet(barrier, who)
    for dx, dz in line:
        greet(barrier, chip_id(dx, dz))

    def loads(b):
        at = pl.ds(start_row(x, b), rows)
        to = pl.ds(start_row(x, b) + PAD, rows)
        return (
            pltpu.make_async_copy(fields.at[:, :, at, :], u.at[:, :, to, :], in_sem.at[b, 0]),
            pltpu.make_async_copy(cond.at[:, at, :], k.at[:, to, :], in_sem.at[b, 1]),
            pltpu.make_async_copy(absn.at[:, at, :], ab.at[:, at, :], in_sem.at[b, 2]),
        )

    for b in range(nb):
        for c in loads(b)[:2]:
            c.start()
    for b in range(nb):
        loads(b)[2].start()

    for p in range(cx):
        k[p, 0:PAD, :] = jnp.zeros((PAD, 128), jnp.float32)
        k[p, PAD + ny : 2 * PAD + ny, :] = jnp.zeros((PAD, 128), jnp.float32)
        for a in range(3):
            u[a, p, 0:PAD, :] = jnp.zeros((PAD, 128), jnp.float32)
            u[a, p, PAD + ny : 2 * PAD + ny, :] = jnp.zeros((PAD, 128), jnp.float32)

    @pl.when(bx == 0)
    def _():
        lo_u[...] = jnp.zeros_like(lo_u)
        lo_k[...] = jnp.zeros_like(lo_k)

    @pl.when(bx == n_bx - 1)
    def _():
        hi_u[...] = jnp.zeros_like(hi_u)
        hi_k[...] = jnp.zeros_like(hi_k)

    @pl.when(bz == 0)
    def _():
        zl[...] = jnp.zeros_like(zl)

    @pl.when(bz == n_bz - 1)
    def _():
        zr[...] = jnp.zeros_like(zr)

    lane = lax.broadcasted_iota(jnp.int32, (8, 128), 1)
    slot = ((lane + 1) % 128) // 2

    def edge(b, right):
        return pltpu.make_async_remote_copy(
            zs.at[b], (zl if right else zr).at[b], zs_sem.at[b, int(right)], zr_sem.at[b, int(right)],
            device_id=r_id if right else l_id, device_id_type=MESH)

    def pack_batch(b):
        for c in loads(b)[:2]:
            c.wait()
        r0 = start_row(x, b)

        def pack(g, carry):
            for h in range(PU):
                row = pl.multiple_of(g * (8 * PU), 8) + h * 8
                at = pl.ds(r0 + row + PAD, 8)
                parts = []
                for a in range(3):
                    out = jnp.zeros((8, 128), jnp.float32)
                    for p in range(cx):
                        j = 3 * p + a
                        v = u[a, p, at, :]
                        out = jnp.where(slot == j, pltpu.roll(v, 2 * j, 1) if j else v, out)
                    parts.append(out)
                out = jnp.zeros((8, 128), jnp.float32)
                for p in range(cx):
                    out = jnp.where(slot == 32 + 3 * p, pltpu.roll(k[p, at, :], 64 + 6 * p, 1), out)
                out = out + pltpu.roll(out, 2, 1) + pltpu.roll(out, 4, 1)
                zs[b, pl.ds(row, 8), :] = (parts[0] + parts[1]) + (parts[2] + out)
            return carry

        lax.fori_loop(0, groups // PU, pack, 0)

    def send_edges(b):
        @pl.when(has_l)
        def _():
            edge(b, False).start()

        @pl.when(has_r)
        def _():
            edge(b, True).start()

    first, last = lane == 0, lane == 127
    rim = first | last
    for b in range(min(EARLY, nb)):
        pack_batch(b)

    pl.semaphore_wait(
        barrier,
        len(line) + has_lo.astype(jnp.int32) + has_hi.astype(jnp.int32)
        + has_l.astype(jnp.int32) + has_r.astype(jnp.int32),
    )

    def halo(b, up):
        of_x, who, p = (hi_x, hi_id, cx - 1) if up else (lo_x, lo_id, 0)
        to_u, to_k = (lo_u, lo_k) if up else (hi_u, hi_k)
        at = pl.ds(start_row(of_x, b), rows)
        d = int(up)
        return (
            pltpu.make_async_remote_copy(
                fields.at[:, p, at, :], to_u.at[:, at, :], hs_sem.at[b, d, 0], hr_sem.at[b, d, 0],
                device_id=who, device_id_type=MESH),
            pltpu.make_async_remote_copy(
                cond.at[p, at, :], to_k.at[at, :], hs_sem.at[b, d, 1], hr_sem.at[b, d, 1],
                device_id=who, device_id_type=MESH),
        )

    for b in range(nb):
        @pl.when(has_lo)
        def _():
            for c in halo(b, False):
                c.start()

        @pl.when(has_hi)
        def _():
            for c in halo(b, True):
                c.start()

    for b in range(min(EARLY, nb)):
        send_edges(b)

    for dx, dz in line:
        greet(word, chip_id(dx, dz))

    flag_loads = [
        pltpu.make_async_copy(ref, flags.at[i], flag_sem.at[i]) for i, ref in enumerate((occ, facing))
    ]
    for c in flag_loads:
        c.start()

    def pack_rest(b, carry):
        pack_batch(b)
        send_edges(b)
        return carry

    if EARLY < nb:
        lax.fori_loop(EARLY, nb, pack_rest, 0)

    for c in flag_loads:
        c.wait()
    occ_m[...] = spread(flags[0])
    fac_m[...] = spread(flags[1])

    def interior(i, carry):
        for h in range(AU):
            y0 = pl.multiple_of(i * (8 * AU), 8) + h * 8
            at = pl.ds(y0, 8)
            mid = pl.ds(y0 + PAD, 8)
            above = pl.ds(y0 + PAD + 1, 8)
            below = pl.ds(y0 + PAD - 1, 8)
            k_here = k[0, mid, :]
            u_here = [u[a, 0, mid, :] for a in range(3)]
            flow = [None] * 3
            for p in range(cx):
                k_a = k_here + k[p, above, :]
                k_b = k_here + k[p, below, :]
                k_r = jnp.where(last, 0.0, k_here + pltpu.roll(k_here, 127, 1))
                if p < cx - 1:
                    k_next = k[p + 1, mid, :]
                    u_next = [u[a, p + 1, mid, :] for a in range(3)]
                    k_x = k_here + k_next
                for a in range(3):
                    v = u_here[a]
                    across = k_r * (pltpu.roll(v, 127, 1) - v)
                    change = across - pltpu.roll(across, 1, 1)
                    change = change + k_a * (u[a, p, above, :] - v)
                    change = change + k_b * (u[a, p, below, :] - v)
                    if p > 0:
                        change = change - flow[a]
                    if p < cx - 1:
                        flow[a] = k_x * (u_next[a] - v)
                        change = change + flow[a]
                    adv[a, p, at, :] = v + change * SHARE
                k_here, u_here = k_next, u_next
        return carry

    lax.fori_loop(0, ny // (8 * AU), interior, 0)
    for b in range(nb):
        loads(b)[2].wait()

    def core_copy(b):
        return pltpu.make_async_remote_copy(
            give.at[b], pair.at[b, core], cs_sem.at[b], cr_sem.at[b], device_id=mate, device_id_type=MESH)

    def send_out(b, i, e):
        far = 4 + ((e + 1) // 2) * (2 * (e % 2) - 1)
        to_x, to_z = ((x // m + b) % nb) * m + i, (z + far) % ZS
        return to_x, pltpu.make_async_remote_copy(
            ready.at[b, i * ZS + to_z], got.at[x * ZS + z], as_sem.at[b, i * ZS + e], ar_sem.at[x * ZS + z],
            device_id=((to_x * ZS + to_z) * 2 + core, bz), device_id_type=MESH)

    def each_out(b, act):
        for e in range(ZS):
            for i in range(m):
                to_x, c = send_out(b, i, e)
                if e < ZS - 1:
                    act(c)
                else:
                    @pl.when(to_x != x)
                    def _():
                        act(c)

    def wait_halo(b):
        @pl.when(has_lo)
        def _():
            for c in halo(b, True):
                c.wait_recv()

        @pl.when(has_hi)
        def _():
            for c in halo(b, False):
                c.wait_recv()

        @pl.when(has_l)
        def _():
            edge(b, True).wait_recv()

        @pl.when(has_r)
        def _():
            edge(b, False).wait_recv()

    def work(b):
        wait_halo(b)
        r0 = start_row(x, b)

        def step(i, carry):
            for h in range(BU):
                row = pl.multiple_of(i * (8 * BU), 8) + h * 8
                g = i * BU + h
                y0 = r0 + row
                at = pl.ds(y0, 8)
                mid = pl.ds(y0 + PAD, 8)
                here = pl.ds(row, 8)
                own = zs[b, here, :]
                other = jnp.where(lane % 2 == 1, pltpu.roll(zr[b, here, :], 127, 1), pltpu.roll(zl[b, here, :], 1, 1))
                into = pltpu.roll(own + other, 64, 1) * (other - own) * SHARE
                tile = y0 // TY
                mask = occ_m[pl.ds(tile, 1), :]
                flip = jnp.broadcast_to(fac_m[pl.ds(tile, 1), :] > 0.5, (8, 128))
                through = jnp.ones((8, 128), jnp.float32)
                colour = [jnp.zeros((8, 128), jnp.float32)] * 3
                for p in range(cx):
                    new = []
                    if p == 0:
                        k_x = (k[0, mid, :] + lo_k[at, :]) * SHARE
                    if p == cx - 1:
                        k_x = (k[p, mid, :] + hi_k[at, :]) * SHARE
                    for a in range(3):
                        j = 3 * p + a
                        out = adv[a, p, at, :]
                        out = out + jnp.where(rim, pltpu.roll(into, 128 - 2 * j, 1) if j else into, 0.0)
                        if p == 0:
                            out = out + k_x * (lo_u[a, at, :] - u[a, p, mid, :])
                        if p == cx - 1:
                            out = out + k_x * (hi_u[a, at, :] - u[a, p, mid, :])
                        adv[a, p, at, :] = out
                        new.append(out)
                    passed = jnp.exp(-(ab[p, at, :] * new[0] * mask))
                    glow = (1.0 - passed) * jnp.where(flip, 1.0, through)
                    keep = jnp.where(flip, passed, 1.0)
                    colour = [colour[a] * keep + new[a] * glow for a in range(3)]
                    through = through * passed
                for c, v in enumerate(colour + [through]):
                    top, bottom = v[0:4], v[4:8]
                    pair[b, core, g, c] = jnp.where(core == 0, top, bottom)
                    give[b, g, c] = jnp.where(core == 0, bottom, top)
            return carry

        lax.fori_loop(0, groups // BU, step, 0)
        core_copy(b).start()

    def merge(b):
        core_copy(b).wait_recv()
        tile0 = (start_row(x, b) // TY)

        def step(g, carry):
            flip = jnp.broadcast_to(fac_m[pl.ds(tile0 + g // 2, 1), :] > 0.5, (4, 128))
            t0, t1 = pair[b, 0, g, 3], pair[b, 1, g, 3]
            for c in range(3):
                c0, c1 = pair[b, 0, g, c], pair[b, 1, g, c]
                ready[b, g, c] = jnp.where(flip, c1 + t1 * c0, c0 + t0 * c1)
            ready[b, g, 3] = t0 * t1
            return carry

        lax.fori_loop(0, groups, step, 0)
        @pl.when(b == 0)
        def _():
            pl.semaphore_wait(word, len(line))

        each_out(b, lambda c: c.start())

    def batch(b, carry):
        @pl.when(b < nb)
        def _():
            work(b)

        @pl.when(b > 0)
        def _():
            merge(b - 1)

        return carry

    lax.fori_loop(0, nb + 1, batch, 0)

    def drain(b, carry):
        @pl.when(has_lo)
        def _():
            for c in halo(b, False):
                c.wait_send()

        @pl.when(has_hi)
        def _():
            for c in halo(b, True):
                c.wait_send()

        @pl.when(has_l)
        def _():
            edge(b, False).wait_send()

        @pl.when(has_r)
        def _():
            edge(b, True).wait_send()

        core_copy(b).wait_send()
        each_out(b, lambda c: c.wait_send())
        return carry

    lax.fori_loop(0, nb, drain, 0)

    flip = jnp.broadcast_to(fac_m[pl.ds(bx * 4 // TY, 1), :] > 0.5, (4, 128))
    me = x * ZS + z
    got[pl.ds(me, 1)] = ready[0, pl.ds(x % m * ZS + z, 1)]

    def gather(s, carry):
        colour, through = carry[:3], carry[3]

        @pl.when(s != me)
        def _():
            pltpu.make_async_remote_copy(
                ready.at[0, 0], got.at[s], as_sem.at[0, 0], ar_sem.at[s],
                device_id=mate, device_id_type=MESH).wait_recv()

        t = got[s, 3]
        colour = [
            jnp.where(flip, got[s, c] + t * colour[c], colour[c] + through * got[s, c]) for c in range(3)
        ]
        return (*colour, through * t)

    zero = jnp.zeros((4, 128), jnp.float32)
    out = lax.fori_loop(0, xs * ZS, gather, (zero, zero, zero, jnp.ones((4, 128), jnp.float32)))
    for c in range(3):
        pic[c] = out[c]
    pic[3] = 1.0 - out[3]


def hand_over(adv, pic, adv_out, pic_out, sem):
    cx = adv.shape[1]
    copies = [pltpu.make_async_copy(adv.at[:, p], adv_out.at[:, p], sem.at[p]) for p in range(cx)]
    copies.append(pltpu.make_async_copy(pic, pic_out, sem.at[cx]))
    for c in copies:
        c.start()
    for c in copies:
        c.wait()


def solution(mesh):
    n_bx, n_bz = mesh.shape["bx"], mesh.shape["bz"]

    def shards(fields, conductance, absorption, occupancy, facing):
        _, cx, ny, nz = fields.shape
        occupancy = occupancy[0].T
        facing = facing.T
        xs = n_bx // (2 * ZS)
        nb, rows = NB, ny // NB
        f32 = jnp.float32
        vmem, dma = pltpu.VMEM, pltpu.SemaphoreType.DMA
        hbm = pl.BlockSpec(memory_space=pltpu.HBM)
        in_vmem = pl.BlockSpec(memory_space=pltpu.VMEM)
        held = pl.pallas_call(
            functools.partial(kernel, n_bx, n_bz, cx, ny),
            out_shape=(
                jax.ShapeDtypeStruct(fields.shape, f32),
                jax.ShapeDtypeStruct((4, ny // n_bx, nz), f32),
            ),
            in_specs=[hbm] * 5,
            out_specs=(in_vmem, in_vmem),
            scratch_shapes=[
                vmem((3, cx, ny + 2 * PAD, nz), f32),
                vmem((cx, ny + 2 * PAD, nz), f32),
                vmem((cx, ny, nz), f32),
                vmem((3, ny, nz), f32),
                vmem((ny, nz), f32),
                vmem((3, ny, nz), f32),
                vmem((ny, nz), f32),
                vmem((nb, rows, nz), f32),
                vmem((nb, rows, nz), f32),
                vmem((nb, rows, nz), f32),
                vmem((ny // TY, nz), f32),
                vmem((ny // TY, nz), f32),
                vmem((nb, 2, rows // 8, 4, 4, nz), f32),
                vmem((nb, rows // 8, 4, 4, nz), f32),
                vmem((nb, rows // 8, 4, 4, nz), f32),
                vmem((xs * ZS, 4, 4, nz), f32),
                vmem((2,) + facing.shape, jnp.int32),
                pltpu.SemaphoreType.REGULAR,
                dma((2,)),
                dma((nb, 3)),
                dma((nb, 2, 2)),
                dma((nb, 2, 2)),
                dma((nb, 2)),
                dma((nb, 2)),
                dma((nb,)),
                dma((nb,)),
                dma((nb, xs // nb * ZS)),
                dma((xs * ZS,)),
            ],
            compiler_params=pltpu.CompilerParams(
                collective_id=0, has_side_effects=True, vmem_limit_bytes=LIMIT
            ),
            name="step_and_render",
        )(*(pltpu.with_memory_space_constraint(v, pltpu.HBM) for v in (fields, conductance, absorption, occupancy, facing)))
        return pl.pallas_call(
            hand_over,
            out_shape=tuple(pltpu.HBM(v.shape, f32) for v in held),
            in_specs=[in_vmem, in_vmem],
            out_specs=(hbm, hbm),
            scratch_shapes=[dma((cx + 1,))],
            name="hand_over",
        )(*(pltpu.with_memory_space_constraint(v, pltpu.VMEM) for v in held))

    return jax.shard_map(
        shards,
        mesh=mesh,
        in_specs=(
            P(None, "bx", None, "bz"),
            P("bx", None, "bz"),
            P("bx", None, "bz"),
            P("bx", None, "bz"),
            P(None, "bz"),
        ),
        out_specs=(P(None, "bx", None, "bz"), P(None, "bx", "bz")),
        check_vma=False,
    )
```

time: 38.7 us -> 29.5 us (0.76)
  local copies, waits for them, and re-layouts: 8.12 us -> 0 us
  Pallas kernels: 29.7 us -> 28.8 us
    unnamed x10 -> x0, local copies, waits for them, and re-layouts: 8.12 us -> none
    pallas_call x1, Pallas kernels: 29.7 us -> 27.1 us  [shards(): pl.pallas_call(functools.partial(kernel, n_bx, n_bz, cx, ny), out_shape=(...]
    pallas_call x0 -> x1, Pallas kernels: none -> 1.73 us  [shards(): pl.pallas_call(hand_over, out_shape=tuple((pltpu.HBM(v.shape, f32) for v...]
where the time goes in v2:
time: 29.5 us; the launch traced here: 29.4 us
  Pallas kernels  28.8 us (98%)
  between operations  0.64 us (2%)
    pallas_call x1, Pallas kernels, shards(): pl.pallas_call(functools.partial(kernel, n_bx, n_bz, cx, ny), out_shape=(...  27.1 us
    pallas_call x1, Pallas kernels, shards(): pl.pallas_call(hand_over, out_shape=tuple((pltpu.HBM(v.shape, f32) for v...  1.73 us

profile of v2, /device:TPU:1, one launch (start us, length us, event | category | flops | bytes accessed | tf_op | source)
XLA Modules:
  0.0 29.4 jit_solution(6292623144008952873)
XLA Ops:
  0.6 27.1 %step_and_render.1 = (f32[3,8,256,128]{3,2,1,0:T(8,128)S(1)}, f32[4,4,128]{2,1,0:T(4,128)S(1)}) custom-call(f32[3,8,256,128]{3,2,1,0:T(8,128)} %fields.1, f32[8,256,128]{2,1,0:T(8,128)} %cond.1, f32[8,256,128]{2,1,0:T(8,128)} %absn.1, s32[4,16]{1,0:T(4,128)} %bitcast.4, s32[4,16]{1,0:T(4,128)} %bitcast.5), custom_call_target="tpu_custom_call" | custom-call | tf_op jit(solution)/shard_map/step_and_render/pallas_call | solution.py:520
  27.7 1.7 %hand_over.1 = (f32[3,8,256,128]{3,2,1,0:T(8,128)}, f32[4,4,128]{2,1,0:T(4,128)}) custom-call(f32[3,8,256,128]{3,2,1,0:T(8,128)S(1)} %get-tuple-element.4.adv, f32[4,4,128]{2,1,0:T(4,128)S(1)} %get-tuple-element.5.pic), custom_call_target="tpu_custom_call" | custom-call | tf_op jit(solution)/shard_map/hand_over/pallas_call | solution.py:563

commit v3 on v2

v3 whole, which is shorter than its diff:
```python
import functools

import jax
import jax.numpy as jnp
from jax import lax
from jax.experimental import pallas as pl
from jax.experimental.pallas import tpu as pltpu
from jax.sharding import PartitionSpec as P

MESH = pl.DeviceIdType.MESH
TY = 16
TZ = 32
ZS = 8
PAD = 8
LIMIT = 30 << 20
SHARE = 0.5 / 7.0
UB = 2
PU, AU, BU = 2, 2, 4
SPLIT = 10
EARLY = 1


def spread(flags):
    column = lax.broadcasted_iota(jnp.int32, (flags.shape[0], 128), 0)
    lane = lax.broadcasted_iota(jnp.int32, (flags.shape[0], 128), 1)
    own = (lane // TZ == column).astype(jnp.float32)
    return lax.dot_general(
        flags.astype(jnp.float32), own, (((0,), (0,)), ((), ())), preferred_element_type=jnp.float32
    )


def kernel(
    n_bx, n_bz, cx, ny,
    fields, cond, absn, occ, facing,
    adv, pic,
    u, k, ab, lo, hi, zs, zl, zr, occ_m, fac_m, pair, give, ready, got, flags,
    word, flag_sem, in_sem, hs_sem, hr_sem, zs_sem, zr_sem, cs_sem, cr_sem, as_sem, ar_sem,
):
    xs = n_bx // (2 * ZS)
    nb = ZS // UB
    groups = UB * xs
    bx = lax.axis_index("bx")
    bz = lax.axis_index("bz")
    core = bx % 2
    z = (bx // 2) % ZS
    x = bx // (2 * ZS)
    has_lo, has_hi = bx > 0, bx < n_bx - 1
    has_l, has_r = bz > 0, bz < n_bz - 1
    lo_id, hi_id = (bx - 1, bz), (bx + 1, bz)
    l_id, r_id = (bx, bz - 1), (bx, bz + 1)
    mate = (bx + 1 - 2 * core, bz)

    def chip_id(dx, dz):
        return ((((x + dx) % xs) * ZS + (z + dz) % ZS) * 2 + core, bz)

    def first_row(i, q):
        return pl.multiple_of(i * (8 * ZS) + q * 8, 8)

    barrier = pltpu.get_barrier_semaphore()
    line = [(0, dz) for dz in (1, ZS - 1, 2, ZS - 2, 3, ZS - 3, 4)] + [(dx, 0) for dx in range(1, xs)]

    def greet(sem, who):
        pl.semaphore_signal(sem, inc=1, device_id=who, device_id_type=MESH)

    for near, who in ((has_lo, lo_id), (has_hi, hi_id), (has_l, l_id), (has_r, r_id)):
        @pl.when(near)
        def _():
            greet(barrier, who)
    for dx, dz in line:
        greet(barrier, chip_id(dx, dz))

    body = pl.ds(PAD, ny)
    loads = [pltpu.make_async_copy(fields.at[a], u.at[a, :, body, :], in_sem.at[a]) for a in range(3)]
    loads.append(pltpu.make_async_copy(cond, k.at[:, body, :], in_sem.at[3]))
    late_load = pltpu.make_async_copy(absn, ab, in_sem.at[4])
    for c in loads:
        c.start()

    lane = lax.broadcasted_iota(jnp.int32, (8, 128), 1)
    first, last = lane == 0, lane == 127
    rim = first | last

    slot = ((lane + 1) % 128) // 2

    def edge(b, right):
        return pltpu.make_async_remote_copy(
            zs.at[b], (zl if right else zr).at[b], zs_sem.at[int(right)],
            zr_sem.at[b, int(right)], device_id=r_id if right else l_id, device_id_type=MESH)

    def pack_batch(b):
        def pack(g, carry):
            for h in range(PU):
                r = g * PU + h
                q, i = b * UB + r // xs, r % xs
                at = pl.ds(first_row(i, q) + PAD, 8)
                parts = []
                for a in range(3):
                    out = jnp.zeros((8, 128), jnp.float32)
                    for p in range(cx):
                        j = 3 * p + a
                        v = u[a, p, at, :]
                        out = jnp.where(slot == j, pltpu.roll(v, 2 * j, 1) if j else v, out)
                    parts.append(out)
                out = jnp.zeros((8, 128), jnp.float32)
                for p in range(cx):
                    out = jnp.where(slot == 32 + 3 * p, pltpu.roll(k[p, at, :], 64 + 6 * p, 1), out)
                out = out + pltpu.roll(out, 2, 1) + pltpu.roll(out, 4, 1)
                zs[b, i, pl.ds(pl.multiple_of(r // xs * 8, 8), 8), :] = (parts[0] + parts[1]) + (parts[2] + out)
            return carry

        lax.fori_loop(0, groups // PU, pack, 0)

    def send_edges(b):
        @pl.when(has_l)
        def _():
            edge(b, False).start()

        @pl.when(has_r)
        def _():
            edge(b, True).start()

    if EARLY:
        for c in loads:
            c.wait()
    for b in range(EARLY):
        pack_batch(b)
    pl.semaphore_wait(
        barrier,
        len(line) + has_lo.astype(jnp.int32) + has_hi.astype(jnp.int32)
        + has_l.astype(jnp.int32) + has_r.astype(jnp.int32),
    )

    def halo(b, up):
        who, p = (hi_id, cx - 1) if up else (lo_id, 0)
        to = lo if up else hi
        d = int(up)
        return (
            pltpu.make_async_remote_copy(
                fields.reshape(3, cx, xs, nb, UB * 8, 128).at[:, p, :, b], to.at[b, 0:3],
                hs_sem.at[d], hr_sem.at[b, d], device_id=who, device_id_type=MESH),
            pltpu.make_async_remote_copy(
                cond.reshape(cx, xs, nb, UB * 8, 128).at[p, :, b], to.at[b, 3],
                hs_sem.at[d], hr_sem.at[b, d], device_id=who, device_id_type=MESH),
        )

    def take(ref, sem):
        pltpu.make_async_copy(ref, ref, sem).wait()

    def each_halo(b, up, act):
        @pl.when(has_hi if up else has_lo)
        def _():
            for c in halo(b, up):
                act(c)

    def send_halo(b, carry):
        each_halo(b, False, lambda c: c.start())
        each_halo(b, True, lambda c: c.start())
        return carry

    lax.fori_loop(0, 1, send_halo, 0)
    for b in range(EARLY):
        send_edges(b)
    lax.fori_loop(1, nb, send_halo, 0)
    for dx, dz in line:
        greet(word, chip_id(dx, dz))

    flag_loads = [
        pltpu.make_async_copy(ref, flags.at[i], flag_sem.at[i]) for i, ref in enumerate((occ, facing))
    ]
    late_load.start()
    for c in flag_loads:
        c.start()
    if not EARLY:
        for c in loads:
            c.wait()

    def pack_rest(b, carry):
        pack_batch(b)
        send_edges(b)
        return carry

    if EARLY < nb:
        lax.fori_loop(EARLY, nb, pack_rest, 0)

    for p in range(cx):
        k[p, 0:PAD, :] = jnp.zeros((PAD, 128), jnp.float32)
        k[p, PAD + ny : 2 * PAD + ny, :] = jnp.zeros((PAD, 128), jnp.float32)
        for a in range(3):
            u[a, p, 0:PAD, :] = jnp.zeros((PAD, 128), jnp.float32)
            u[a, p, PAD + ny : 2 * PAD + ny, :] = jnp.zeros((PAD, 128), jnp.float32)

    @pl.when(bx == 0)
    def _():
        lo[...] = jnp.zeros_like(lo)

    @pl.when(bx == n_bx - 1)
    def _():
        hi[...] = jnp.zeros_like(hi)

    @pl.when(bz == 0)
    def _():
        zl[...] = jnp.zeros_like(zl)

    @pl.when(bz == n_bz - 1)
    def _():
        zr[...] = jnp.zeros_like(zr)

    for c in flag_loads:
        c.wait()
    occ_m[...] = spread(flags[0])
    fac_m[...] = spread(flags[1])

    def interior(n, carry):
        for h in range(AU):
            r = n * AU + h
            y0 = first_row(r // UB % xs, r // groups * UB + r % UB)
            at = pl.ds(y0, 8)
            mid = pl.ds(y0 + PAD, 8)
            above = pl.ds(y0 + PAD + 1, 8)
            below = pl.ds(y0 + PAD - 1, 8)
            k_here = k[0, mid, :]
            u_here = [u[a, 0, mid, :] for a in range(3)]
            flow = [None] * 3
            for p in range(cx):
                k_a = k_here + k[p, above, :]
                k_b = k_here + k[p, below, :]
                k_r = jnp.where(last, 0.0, k_here + pltpu.roll(k_here, 127, 1))
                if p < cx - 1:
                    k_next = k[p + 1, mid, :]
                    u_next = [u[a, p + 1, mid, :] for a in range(3)]
                    k_x = k_here + k_next
                for a in range(3):
                    v = u_here[a]
                    across = k_r * (pltpu.roll(v, 127, 1) - v)
                    change = across - pltpu.roll(across, 1, 1)
                    change = change + k_a * (u[a, p, above, :] - v)
                    change = change + k_b * (u[a, p, below, :] - v)
                    if p > 0:
                        change = change - flow[a]
                    if p < cx - 1:
                        flow[a] = k_x * (u_next[a] - v)
                        change = change + flow[a]
                    adv[a, p, at, :] = v + change * SHARE
                k_here, u_here = k_next, u_next
        return carry

    lax.fori_loop(0, SPLIT, interior, 0)
    late_load.wait()

    def core_copy(b):
        units = pl.ds(b * UB, UB)
        return pltpu.make_async_remote_copy(
            give.at[units], pair.at[core, units], cs_sem, cr_sem.at[b],
            device_id=mate, device_id_type=MESH)

    def send_out(q, dx):
        to_x = (x + dx) % xs
        return pltpu.make_async_remote_copy(
            ready.at[q, to_x], got.at[x * ZS + z], as_sem, ar_sem,
            device_id=((to_x * ZS + q) * 2 + core, bz), device_id_type=MESH)

    def each_out(q, act):
        for dx in (2, 1, 3):
            act(send_out(q, dx))

        @pl.when(q != z)
        def _():
            act(send_out(q, 0))

    def work(b):
        @pl.when(has_lo)
        def _():
            take(lo.at[b], hr_sem.at[b, 1])

        @pl.when(has_hi)
        def _():
            take(hi.at[b], hr_sem.at[b, 0])

        @pl.when(has_l)
        def _():
            edge(b, True).wait_recv()

        @pl.when(has_r)
        def _():
            edge(b, False).wait_recv()

        def step(n, carry):
            for h in range(BU):
                r = n * BU + h
                q, i = b * UB + r // xs, r % xs
                y0 = first_row(i, q)
                at = pl.ds(y0, 8)
                mid = pl.ds(y0 + PAD, 8)
                here = pl.ds(pl.multiple_of(r // xs * 8, 8), 8)
                own = zs[b, i, here, :]
                other = jnp.where(lane % 2 == 1, pltpu.roll(zr[b, i, here, :], 127, 1), pltpu.roll(zl[b, i, here, :], 1, 1))
                into = pltpu.roll(own + other, 64, 1) * (other - own) * SHARE
                tile = y0 // TY
                mask = occ_m[pl.ds(tile, 1), :]
                flip = jnp.broadcast_to(fac_m[pl.ds(tile, 1), :] > 0.5, (8, 128))
                through = jnp.ones((8, 128), jnp.float32)
                colour = [jnp.zeros((8, 128), jnp.float32)] * 3
                for p in range(cx):
                    new = []
                    if p == 0:
                        k_x = (k[0, mid, :] + lo[b, 3, i, here, :]) * SHARE
                    if p == cx - 1:
                        k_x = (k[p, mid, :] + hi[b, 3, i, here, :]) * SHARE
                    for a in range(3):
                        j = 3 * p + a
                        out = adv[a, p, at, :]
                        out = out + jnp.where(rim, pltpu.roll(into, 128 - 2 * j, 1) if j else into, 0.0)
                        if p == 0:
                            out = out + k_x * (lo[b, a, i, here, :] - u[a, p, mid, :])
                        if p == cx - 1:
                            out = out + k_x * (hi[b, a, i, here, :] - u[a, p, mid, :])
                        adv[a, p, at, :] = out
                        new.append(out)
                    passed = jnp.exp(-(ab[p, at, :] * new[0] * mask))
                    glow = (1.0 - passed) * jnp.where(flip, 1.0, through)
                    keep = jnp.where(flip, passed, 1.0)
                    colour = [colour[a] * keep + new[a] * glow for a in range(3)]
                    through = through * passed
                for c, v in enumerate(colour + [through]):
                    top, bottom = v[0:4], v[4:8]
                    pair[core, q, i, c] = jnp.where(core == 0, top, bottom)
                    give[q, i, c] = jnp.where(core == 0, bottom, top)
            return carry

        lax.fori_loop(0, groups // BU, step, 0)
        core_copy(b).start()

    def merge(b):
        core_copy(b).wait_recv()

        def step(r, carry):
            q, i = b * UB + r // xs, r % xs
            flip = jnp.broadcast_to(fac_m[pl.ds(first_row(i, q) // TY, 1), :] > 0.5, (4, 128))
            t0, t1 = pair[0, q, i, 3], pair[1, q, i, 3]
            for c in range(3):
                c0, c1 = pair[0, q, i, c], pair[1, q, i, c]
                ready[q, i, c] = jnp.where(flip, c1 + t1 * c0, c0 + t0 * c1)
            ready[q, i, 3] = t0 * t1
            return carry

        lax.fori_loop(0, groups, step, 0)

        @pl.when(b == 0)
        def _():
            pl.semaphore_wait(word, len(line))

        for v in range(UB):
            each_out(b * UB + v, lambda c: c.start())

    def batch(n, carry):
        @pl.when(n < nb)
        def _():
            work(n)

        @pl.when(n == 0)
        def _():
            lax.fori_loop(SPLIT, ny // (8 * AU), interior, 0)

        @pl.when(n != 1)
        def _():
            merge(jnp.maximum(n - 1, 0))

        return carry

    lax.fori_loop(0, nb + 1, batch, 0)

    @pl.when(has_lo)
    def _():
        take(hi, hs_sem.at[0])

    @pl.when(has_hi)
    def _():
        take(lo, hs_sem.at[1])

    @pl.when(has_l)
    def _():
        take(zs, zs_sem.at[0])

    @pl.when(has_r)
    def _():
        take(zs, zs_sem.at[1])

    take(give, cs_sem)
    others = got.at[pl.ds(0, xs * ZS - 1)]
    take(others, as_sem)

    flip = jnp.broadcast_to(fac_m[pl.ds(bx * 4 // TY, 1), :] > 0.5, (4, 128))
    me = x * ZS + z
    got[pl.ds(me, 1)] = ready[pl.ds(z, 1), x]

    take(others, ar_sem)

    def gather(s, carry):
        colour, through = list(carry[:3]), carry[3]
        for h in range(ZS):
            t = got[s * ZS + h, 3]
            for c in range(3):
                piece = got[s * ZS + h, c]
                colour[c] = jnp.where(flip, piece + t * colour[c], colour[c] + through * piece)
            through = through * t
        return (*colour, through)

    zero = jnp.zeros((4, 128), jnp.float32)
    out = lax.fori_loop(0, xs, gather, (zero, zero, zero, jnp.ones((4, 128), jnp.float32)))
    for c in range(3):
        pic[c] = out[c]
    pic[3] = 1.0 - out[3]


def hand_over(adv, pic, adv_out, pic_out, sem):
    cx = adv.shape[1]
    copies = [pltpu.make_async_copy(adv.at[:, p], adv_out.at[:, p], sem.at[p]) for p in range(cx)]
    copies.append(pltpu.make_async_copy(pic, pic_out, sem.at[cx]))
    for c in copies:
        c.start()
    for c in copies:
        c.wait()


def solution(mesh):
    n_bx, n_bz = mesh.shape["bx"], mesh.shape["bz"]

    def shards(fields, conductance, absorption, occupancy, facing):
        _, cx, ny, nz = fields.shape
        occupancy = occupancy[0].T
        facing = facing.T
        xs, nb = n_bx // (2 * ZS), ZS // UB
        f32 = jnp.float32
        vmem, dma = pltpu.VMEM, pltpu.SemaphoreType.DMA
        hbm = pl.BlockSpec(memory_space=pltpu.HBM)
        in_vmem = pl.BlockSpec(memory_space=pltpu.VMEM)
        operands = (fields, conductance, absorption, occupancy, facing)
        held = pl.pallas_call(
            functools.partial(kernel, n_bx, n_bz, cx, ny),
            out_shape=(
                jax.ShapeDtypeStruct(fields.shape, f32),
                jax.ShapeDtypeStruct((4, ny // n_bx, nz), f32),
            ),
            in_specs=[hbm] * 5,
            out_specs=(in_vmem, in_vmem),
            scratch_shapes=[
                vmem((3, cx, ny + 2 * PAD, nz), f32),
                vmem((cx, ny + 2 * PAD, nz), f32),
                vmem((cx, ny, nz), f32),
                vmem((nb, 4, xs, UB * 8, nz), f32),
                vmem((nb, 4, xs, UB * 8, nz), f32),
                vmem((nb, xs, UB * 8, nz), f32),
                vmem((nb, xs, UB * 8, nz), f32),
                vmem((nb, xs, UB * 8, nz), f32),
                vmem((ny // TY, nz), f32),
                vmem((ny // TY, nz), f32),
                vmem((2, ZS, xs, 4, 4, nz), f32),
                vmem((ZS, xs, 4, 4, nz), f32),
                vmem((ZS, xs, 4, 4, nz), f32),
                vmem((xs * ZS, 4, 4, nz), f32),
                vmem((2,) + facing.shape, jnp.int32),
                pltpu.SemaphoreType.REGULAR,
                dma((2,)),
                dma((5,)),
                dma((2,)),
                dma((nb, 2)),
                dma((2,)),
                dma((nb, 2)),
                dma(()),
                dma((nb,)),
                dma(()),
                dma(()),
            ],
            compiler_params=pltpu.CompilerParams(
                collective_id=0, has_side_effects=True, vmem_limit_bytes=LIMIT
            ),
            name="step_and_render",
        )(*(pltpu.with_memory_space_constraint(v, pltpu.HBM) for v in operands))
        return pl.pallas_call(
            hand_over,
            out_shape=tuple(pltpu.HBM(v.shape, f32) for v in held),
            in_specs=[in_vmem, in_vmem],
            out_specs=(hbm, hbm),
            scratch_shapes=[dma((cx + 1,))],
            name="hand_over",
        )(*(pltpu.with_memory_space_constraint(v, pltpu.VMEM) for v in held))

    return jax.shard_map(
        shards,
        mesh=mesh,
        in_specs=(
            P(None, "bx", None, "bz"),
            P("bx", None, "bz"),
            P("bx", None, "bz"),
            P("bx", None, "bz"),
            P(None, "bz"),
        ),
        out_specs=(P(None, "bx", None, "bz"), P(None, "bx", "bz")),
        check_vma=False,
    )
```

time: 29.5 us -> 27.6 us (0.936)
  Pallas kernels: 28.8 us -> 26.9 us
    pallas_call x1, Pallas kernels: 27.1 us -> 25.1 us  [shards(): pl.pallas_call(functools.partial(kernel, n_bx, n_bz, cx, ny), out_shape=(...]
where the time goes in v3:
time: 27.6 us; the launch traced here: 27.5 us
  Pallas kernels  26.9 us (97%)
  between operations  0.64 us (2%)
    pallas_call x1, Pallas kernels, shards(): pl.pallas_call(functools.partial(kernel, n_bx, n_bz, cx, ny), out_shape=(...  25.1 us
    pallas_call x1, Pallas kernels, shards(): pl.pallas_call(hand_over, out_shape=tuple((pltpu.HBM(v.shape, f32) for v...  1.73 us

profile of v3, /device:TPU:1, one launch (start us, length us, event | category | flops | bytes accessed | tf_op | source)
XLA Modules:
  0.0 27.5 jit_solution(4031119456493027197)
XLA Ops:
  0.6 25.1 %step_and_render.1 = (f32[3,8,256,128]{3,2,1,0:T(8,128)S(1)}, f32[4,4,128]{2,1,0:T(4,128)S(1)}) custom-call(f32[3,8,256,128]{3,2,1,0:T(8,128)} %fields.1, f32[8,256,128]{2,1,0:T(8,128)} %cond.1, f32[8,256,128]{2,1,0:T(8,128)} %absn.1, s32[4,16]{1,0:T(4,128)} %bitcast.4, s32[4,16]{1,0:T(4,128)} %bitcast.5), custom_call_target="tpu_custom_call" | custom-call | tf_op jit(solution)/shard_map/step_and_render/pallas_call | solution.py:438
  25.8 1.7 %hand_over.1 = (f32[3,8,256,128]{3,2,1,0:T(8,128)}, f32[4,4,128]{2,1,0:T(4,128)}) custom-call(f32[3,8,256,128]{3,2,1,0:T(8,128)S(1)} %get-tuple-element.4.adv, f32[4,4,128]{2,1,0:T(4,128)S(1)} %get-tuple-element.5.pic), custom_call_target="tpu_custom_call" | custom-call | tf_op jit(solution)/shard_map/hand_over/pallas_call | solution.py:479

commit v4 on v3

--- a/solution.py
+++ b/solution.py
@@ -15,7 +15,7 @@
 LIMIT = 30 << 20
 SHARE = 0.5 / 7.0
 UB = 2
-PU, AU, BU = 2, 2, 4
+PU, AU, BU = 4, 2, 8
 SPLIT = 10
 EARLY = 1
 
@@ -73,7 +73,10 @@
     loads = [pltpu.make_async_copy(fields.at[a], u.at[a, :, body, :], in_sem.at[a]) for a in range(3)]
     loads.append(pltpu.make_async_copy(cond, k.at[:, body, :], in_sem.at[3]))
     late_load = pltpu.make_async_copy(absn, ab, in_sem.at[4])
-    for c in loads:
+    flag_loads = [
+        pltpu.make_async_copy(ref, flags.at[i], flag_sem.at[i]) for i, ref in enumerate((occ, facing))
+    ]
+    for c in flag_loads + loads:
         c.start()
 
     lane = lax.broadcasted_iota(jnp.int32, (8, 128), 1)
@@ -119,6 +122,34 @@
         def _():
             edge(b, True).start()
 
+    for p in range(cx):
+        k[p, 0:PAD, :] = jnp.zeros((PAD, 128), jnp.float32)
+        k[p, PAD + ny : 2 * PAD + ny, :] = jnp.zeros((PAD, 128), jnp.float32)
+        for a in range(3):
+            u[a, p, 0:PAD, :] = jnp.zeros((PAD, 128), jnp.float32)
+            u[a, p, PAD + ny : 2 * PAD + ny, :] = jnp.zeros((PAD, 128), jnp.float32)
+
+    @pl.when(bx == 0)
+    def _():
+        lo[...] = jnp.zeros_like(lo)
+
+    @pl.when(bx == n_bx - 1)
+    def _():
+        hi[...] = jnp.zeros_like(hi)
+
+    @pl.when(bz == 0)
+    def _():
+        zl[...] = jnp.zeros_like(zl)
+
+    @pl.when(bz == n_bz - 1)
+    def _():
+        zr[...] = jnp.zeros_like(zr)
+
+    for c in flag_loads:
+        c.wait()
+    occ_m[...] = spread(flags[0])
+    fac_m[...] = spread(flags[1])
+
     if EARLY:
         for c in loads:
             c.wait()
@@ -164,12 +195,7 @@
     for dx, dz in line:
         greet(word, chip_id(dx, dz))
 
-    flag_loads = [
-        pltpu.make_async_copy(ref, flags.at[i], flag_sem.at[i]) for i, ref in enumerate((occ, facing))
-    ]
     late_load.start()
-    for c in flag_loads:
-        c.start()
     if not EARLY:
         for c in loads:
             c.wait()
@@ -181,34 +207,6 @@
 
     if EARLY < nb:
         lax.fori_loop(EARLY, nb, pack_rest, 0)
-
-    for p in range(cx):
-        k[p, 0:PAD, :] = jnp.zeros((PAD, 128), jnp.float32)
-        k[p, PAD + ny : 2 * PAD + ny, :] = jnp.zeros((PAD, 128), jnp.float32)
-        for a in range(3):
-            u[a, p, 0:PAD, :] = jnp.zeros((PAD, 128), jnp.float32)
-            u[a, p, PAD + ny : 2 * PAD + ny, :] = jnp.zeros((PAD, 128), jnp.float32)
-
-    @pl.when(bx == 0)
-    def _():
-        lo[...] = jnp.zeros_like(lo)
-
-    @pl.when(bx == n_bx - 1)
-    def _():
-        hi[...] = jnp.zeros_like(hi)
-
-    @pl.when(bz == 0)
-    def _():
-        zl[...] = jnp.zeros_like(zl)
-
-    @pl.when(bz == n_bz - 1)
-    def _():
-        zr[...] = jnp.zeros_like(zr)
-
-    for c in flag_loads:
-        c.wait()
-    occ_m[...] = spread(flags[0])
-    fac_m[...] = spread(flags[1])
 
     def interior(n, carry):
         for h in range(AU):
@@ -333,17 +331,18 @@
     def merge(b):
         core_copy(b).wait_recv()
 
-        def step(r, carry):
-            q, i = b * UB + r // xs, r % xs
-            flip = jnp.broadcast_to(fac_m[pl.ds(first_row(i, q) // TY, 1), :] > 0.5, (4, 128))
-            t0, t1 = pair[0, q, i, 3], pair[1, q, i, 3]
-            for c in range(3):
-                c0, c1 = pair[0, q, i, c], pair[1, q, i, c]
-                ready[q, i, c] = jnp.where(flip, c1 + t1 * c0, c0 + t0 * c1)
-            ready[q, i, 3] = t0 * t1
+        def step(v, carry):
+            q = b * UB + v
+            for i in range(xs):
+                flip = jnp.broadcast_to(fac_m[pl.ds(first_row(i, q) // TY, 1), :] > 0.5, (4, 128))
+                t0, t1 = pair[0, q, i, 3], pair[1, q, i, 3]
+                for c in range(3):
+                    c0, c1 = pair[0, q, i, c], pair[1, q, i, c]
+                    ready[q, i, c] = jnp.where(flip, c1 + t1 * c0, c0 + t0 * c1)
+                ready[q, i, 3] = t0 * t1
             return carry
 
-        lax.fori_loop(0, groups, step, 0)
+        lax.fori_loop(0, UB, step, 0)
 
         @pl.when(b == 0)
         def _():

time: 27.6 us -> 26.5 us (0.960)
  Pallas kernels: 26.9 us -> 25.8 us
    pallas_call x1, Pallas kernels: 25.1 us -> 24 us  [shards(): pl.pallas_call(functools.partial(kernel, n_bx, n_bz, cx, ny), out_shape=(...]
where the time goes in v4:
time: 26.5 us; the launch traced here: 26.4 us
  Pallas kernels  25.8 us (97%)
  between operations  0.64 us (2%)
    pallas_call x1, Pallas kernels, shards(): pl.pallas_call(functools.partial(kernel, n_bx, n_bz, cx, ny), out_shape=(...  24 us
    pallas_call x1, Pallas kernels, shards(): pl.pallas_call(hand_over, out_shape=tuple((pltpu.HBM(v.shape, f32) for v...  1.73 us

profile of v4, /device:TPU:1, one launch (start us, length us, event | category | flops | bytes accessed | tf_op | source)
XLA Modules:
  0.0 26.4 jit_solution(10985680197433087862)
XLA Ops:
  0.6 24.0 %step_and_render.1 = (f32[3,8,256,128]{3,2,1,0:T(8,128)S(1)}, f32[4,4,128]{2,1,0:T(4,128)S(1)}) custom-call(f32[3,8,256,128]{3,2,1,0:T(8,128)} %fields.1, f32[8,256,128]{2,1,0:T(8,128)} %cond.1, f32[8,256,128]{2,1,0:T(8,128)} %absn.1, s32[4,16]{1,0:T(4,128)} %bitcast.4, s32[4,16]{1,0:T(4,128)} %bitcast.5), custom_call_target="tpu_custom_call" | custom-call | tf_op jit(solution)/shard_map/step_and_render/pallas_call | solution.py:437
  24.7 1.7 %hand_over.1 = (f32[3,8,256,128]{3,2,1,0:T(8,128)}, f32[4,4,128]{2,1,0:T(4,128)}) custom-call(f32[3,8,256,128]{3,2,1,0:T(8,128)S(1)} %get-tuple-element.4.adv, f32[4,4,128]{2,1,0:T(4,128)S(1)} %get-tuple-element.5.pic), custom_call_target="tpu_custom_call" | custom-call | tf_op jit(solution)/shard_map/hand_over/pallas_call | solution.py:478
